TPU v7x, 512 devices: a whole 4x4x16 slice. The times are simulated.
512 devices in a mesh: lat: 4 (over y_lo, core), lon: 32 (over y_hi, z), head: 4 (over x).
Axes of the slice: x: 4, y: 4 (y_hi: 2, y_lo: 2; y = y_hi * 2 + y_lo), z: 16, core: 2. Of those that a mesh axis runs over, the one named last changes fastest.
Arguments:
- activations: bfloat16 [32, 1024, 768], P('lat', ('lon', 'head')), may hold values from -6 to 6
- qkv_weight: bfloat16 [3, 768, 768], P(None, 'head'), may hold values from -0.21875 to 0.21875
- out_weight: bfloat16 [768, 768], P('head'), may hold values from -0.21875 to 0.21875
- valid: int32 [32, 1024], P('lat', 'lon'), may hold values 0 or 1
- grad_y: bfloat16 [32, 1024, 768], P('lat', ('lon', 'head')), may hold values from -6 to 6
Outputs:
- mixed: bfloat16 [32, 1024, 768], P('lat', ('lon', 'head'))
- grad_x: bfloat16 [32, 1024, 768], P('lat', ('lon', 'head'))
- grad_qkv_weight: bfloat16 [3, 768, 768], P(None, 'head')
- grad_out_weight: bfloat16 [768, 768], P('head')
All inputs are finite; a program needn't handle non-finite values. No bound on the sum of `valid` on one device may be relied on, other than what follows from the above.
Results may differ from a plain program's by a relative error of at most 0.011.
Values may be sent and summed in bfloat16 or wider, within the bound.
A program may use at most 64 MiB of HBM per device.

v0:
```python
import jax
import jax.numpy as jnp
import numpy as np
from jax import lax
from jax.sharding import PartitionSpec as P

HEAD_SIZE = 64
REACH = 6


TILE_ROWS = 8
TILE_COLS = 16
NEGATIVE = -1e30


def extended(cells, sides, width):
    for axis, dim in sides:
        count = lax.axis_size(axis)
        head = lax.slice_in_dim(cells, 0, width, axis=dim)
        tail = lax.slice_in_dim(cells, cells.shape[dim] - width, cells.shape[dim], axis=dim)
        cells = jnp.concatenate(
            [
                lax.ppermute(tail, axis, [(i, (i + 1) % count) for i in range(count)]),
                cells,
                lax.ppermute(head, axis, [((i + 1) % count, i) for i in range(count)]),
            ],
            axis=dim,
        )
    return cells


def normalize(values):
    wide = values.astype(jnp.float32)
    center = wide - jnp.mean(wide, axis=-1, keepdims=True)
    spread = jnp.mean(center * center, axis=-1, keepdims=True)
    inv_spread = lax.rsqrt(spread + 1e-05)
    return (center * inv_spread, inv_spread)


def window_tables(radius):
    block_rows = TILE_ROWS + 2 * radius
    block_cols = TILE_COLS + 2 * radius
    query_cells = np.arange(TILE_ROWS * TILE_COLS)
    block_cells = np.arange(block_rows * block_cols)
    step_lat = (block_cells // block_cols)[None, :] - radius - (query_cells // TILE_COLS)[:, None]
    step_lon = (block_cells % block_cols)[None, :] - radius - (query_cells % TILE_COLS)[:, None]
    inside = (np.abs(step_lat) <= radius) & (np.abs(step_lon) <= radius)
    center = (step_lat == 0) & (step_lon == 0)
    return (jnp.asarray(inside), jnp.asarray(center))


def cut_block(field, top, left, rows, cols):
    starts = (top, left) + (0,) * (field.ndim - 2)
    piece = lax.dynamic_slice(field, starts, (rows, cols) + field.shape[2:])
    return piece.reshape((rows * cols,) + field.shape[2:])


def untile(pieces, tiles_down, tiles_across):
    rest = pieces.shape[2:]
    grid = pieces.reshape((tiles_down, tiles_across, TILE_ROWS, TILE_COLS) + rest)
    order = (0, 2, 1, 3) + tuple(range(4, grid.ndim))
    return grid.transpose(order).reshape((tiles_down * TILE_ROWS, tiles_across * TILE_COLS) + rest)


def project_rows(normed_rows, weight):
    return lax.dot_general(
        normed_rows, weight, (((1,), (2,)), ((), ())), preferred_element_type=jnp.float32
    )


def on_device(activations, qkv_weight, out_weight, valid, grad_y):
    lat_cells, own_cols, full = activations.shape
    width = qkv_weight.shape[1]
    heads = width // HEAD_SIZE
    scale = HEAD_SIZE ** (-0.5)
    radius = REACH
    block_rows = TILE_ROWS + 2 * radius
    block_cols = TILE_COLS + 2 * radius
    whole = lax.all_gather(activations, "head", axis=1, tiled=True)
    lon_cells = whole.shape[1]
    tiles_down = lat_cells // TILE_ROWS
    tiles_across = lon_cells // TILE_COLS
    tile_ids = jnp.arange(tiles_down * tiles_across, dtype=jnp.int32)
    rows_all = lat_cells * lax.axis_size("lat")
    global_rows = (
        lax.axis_index("lat") * lat_cells
        - radius
        + jnp.arange(lat_cells + 2 * radius, dtype=jnp.int32)
    )
    row_inside = ((global_rows >= 0) & (global_rows < rows_all)).astype(jnp.float32)
    row_margin = jnp.broadcast_to(
        row_inside[:, None], (lat_cells + 2 * radius, lon_cells + 2 * radius)
    )
    valid_half = valid.astype(jnp.bfloat16)
    norm32, inv_spread = normalize(whole)
    normed = norm32.astype(jnp.bfloat16)
    projected = project_rows(normed.reshape(-1, full), qkv_weight)
    projected = projected.astype(jnp.bfloat16).reshape(lat_cells, lon_cells, 3, width)
    query = projected[:, :, 0]
    paired = projected[:, :, 1:].reshape(lat_cells, lon_cells, 2 * width)
    pair_margin, margin_valid = (
        extended(paired, (("lat", 0), ("lon", 1)), REACH),
        extended(valid_half, (("lat", 0), ("lon", 1)), REACH),
    )
    key_margin = pair_margin[:, :, :width]
    value_margin = pair_margin[:, :, width:]
    key_flag = margin_valid.astype(jnp.float32) * row_margin
    inside, center = window_tables(radius)

    def by_heads(piece):
        return piece.reshape(piece.shape[0], heads, HEAD_SIZE)

    def tile_start(index):
        return (index // tiles_across * TILE_ROWS, index % tiles_across * TILE_COLS)

    def forward_tile(index):
        top, left = tile_start(index)
        query_tile = by_heads(cut_block(query, top, left, TILE_ROWS, TILE_COLS))
        key_block = by_heads(cut_block(key_margin, top, left, block_rows, block_cols))
        value_block = by_heads(cut_block(value_margin, top, left, block_rows, block_cols))
        flag_block = cut_block(key_flag, top, left, block_rows, block_cols)
        allowed = inside & ((flag_block[None, :] > 0) | center)
        score = scale * jnp.einsum(
            "qhc,khc->hqk", query_tile, key_block, preferred_element_type=jnp.float32
        )
        score = jnp.where(allowed, score, NEGATIVE)
        best = jnp.max(score, axis=2, keepdims=True)
        total = jnp.sum(jnp.where(allowed, jnp.exp(score - best), 0.0), axis=2, keepdims=True)
        level = best + jnp.log(total)
        soft = jnp.where(allowed, jnp.exp(score - level), 0.0).astype(jnp.bfloat16)
        result = jnp.einsum("hqk,khc->qhc", soft, value_block, preferred_element_type=jnp.float32)
        return (result.astype(jnp.bfloat16).reshape(TILE_ROWS * TILE_COLS, width), level[:, :, 0].T)

    attended_tiles, level_tiles = lax.map(forward_tile, tile_ids)
    attended = untile(attended_tiles, tiles_down, tiles_across)
    level = untile(level_tiles, tiles_down, tiles_across)
    attended_rows = attended.reshape(-1, width)
    partial_value = jnp.dot(attended_rows, out_weight, preferred_element_type=jnp.float32).reshape(
        lat_cells, lon_cells, full
    )
    summed = lax.psum_scatter(
        partial_value.astype(jnp.bfloat16), "head", scatter_dimension=1, tiled=True
    ).astype(jnp.float32)
    mixed = (activations.astype(jnp.float32) + summed).astype(jnp.bfloat16)
    grad_full = lax.all_gather(grad_y, "head", axis=1, tiled=True)
    grad_rows = grad_full.reshape(-1, full)
    grad_out_local = jnp.einsum(
        "nc,nd->cd", attended_rows, grad_rows, preferred_element_type=jnp.float32
    )
    d_attended = jnp.einsum("nd,cd->nc", grad_rows, out_weight, preferred_element_type=jnp.float32)
    d_attended = d_attended.astype(jnp.bfloat16).reshape(lat_cells, lon_cells, width)
    carried = jnp.einsum(
        "xyhc,xyhc->xyh",
        d_attended.reshape(lat_cells, lon_cells, heads, HEAD_SIZE),
        attended.reshape(lat_cells, lon_cells, heads, HEAD_SIZE),
        preferred_element_type=jnp.float32,
    )
    margin_pair = extended(
        jnp.concatenate([query, d_attended], axis=2), (("lat", 0), ("lon", 1)), REACH
    )
    margin_stats = extended(
        jnp.concatenate([level, carried], axis=2), (("lat", 0), ("lon", 1)), REACH
    )
    query_margin = margin_pair[:, :, :width]
    dout_margin = margin_pair[:, :, width:]
    level_margin = margin_stats[:, :, :heads]
    carried_margin = margin_stats[:, :, heads:]
    valid_own = valid.astype(jnp.float32)

    def backward_tile(index):
        top, left = tile_start(index)
        query_tile = by_heads(cut_block(query, top, left, TILE_ROWS, TILE_COLS))
        dout_tile = by_heads(cut_block(d_attended, top, left, TILE_ROWS, TILE_COLS))
        level_tile = cut_block(level, top, left, TILE_ROWS, TILE_COLS)
        carried_tile = cut_block(carried, top, left, TILE_ROWS, TILE_COLS)
        key_block = by_heads(cut_block(key_margin, top, left, block_rows, block_cols))
        value_block = by_heads(cut_block(value_margin, top, left, block_rows, block_cols))
        flag_block = cut_block(key_flag, top, left, block_rows, block_cols)
        allowed = inside & ((flag_block[None, :] > 0) | center)
        score = scale * jnp.einsum(
            "qhc,khc->hqk", query_tile, key_block, preferred_element_type=jnp.float32
        )
        chance = jnp.where(allowed, jnp.exp(score - level_tile.T[:, :, None]), 0.0)
        inner = jnp.einsum(
            "qhc,khc->hqk", dout_tile, value_block, preferred_element_type=jnp.float32
        )
        soft_grad = (chance * (inner - carried_tile.T[:, :, None])).astype(jnp.bfloat16)
        grad_query = scale * jnp.einsum(
            "hqk,khc->qhc", soft_grad, key_block, preferred_element_type=jnp.float32
        )
        key_tile = by_heads(
            cut_block(key_margin, top + radius, left + radius, TILE_ROWS, TILE_COLS)
        )
        value_tile = by_heads(
            cut_block(value_margin, top + radius, left + radius, TILE_ROWS, TILE_COLS)
        )
        own_flag = cut_block(valid_own, top, left, TILE_ROWS, TILE_COLS)
        query_block = by_heads(cut_block(query_margin, top, left, block_rows, block_cols))
        dout_block = by_heads(cut_block(dout_margin, top, left, block_rows, block_cols))
        level_block = cut_block(level_margin, top, left, block_rows, block_cols)
        carried_block = cut_block(carried_margin, top, left, block_rows, block_cols)
        rows_block = cut_block(row_margin, top, left, block_rows, block_cols)
        allowed_keys = inside & ((own_flag[:, None] > 0) | center) & (rows_block[None, :] > 0)
        score_keys = scale * jnp.einsum(
            "khc,qhc->hkq", key_tile, query_block, preferred_element_type=jnp.float32
        )
        chance_keys = jnp.where(allowed_keys, jnp.exp(score_keys - level_block.T[:, None, :]), 0.0)
        inner_keys = jnp.einsum(
            "qhc,khc->hkq", dout_block, value_tile, preferred_element_type=jnp.float32
        )
        soft_grad_keys = (chance_keys * (inner_keys - carried_block.T[:, None, :])).astype(
            jnp.bfloat16
        )
        grad_key = scale * jnp.einsum(
            "hkq,qhc->khc", soft_grad_keys, query_block, preferred_element_type=jnp.float32
        )
        grad_value = jnp.einsum(
            "hkq,qhc->khc",
            chance_keys.astype(jnp.bfloat16),
            dout_block,
            preferred_element_type=jnp.float32,
        )
        stacked = jnp.stack([grad_query, grad_key, grad_value], axis=1).astype(jnp.bfloat16)
        return stacked.reshape(TILE_ROWS * TILE_COLS, 3 * width)

    grad_tiles = lax.map(backward_tile, tile_ids)
    grad_projected = untile(grad_tiles, tiles_down, tiles_across).reshape(-1, 3, width)
    grad_qkv_local = jnp.einsum(
        "nkc,nd->kcd", grad_projected, normed.reshape(-1, full), preferred_element_type=jnp.float32
    )
    grad_qkv_sum, grad_out_sum = lax.psum((grad_qkv_local, grad_out_local), ("lat", "lon"))
    grad_normed = jnp.einsum(
        "nkc,kcd->nd", grad_projected, qkv_weight, preferred_element_type=jnp.float32
    )
    grad_normed = grad_normed.reshape(lat_cells, lon_cells, full)
    start = lax.axis_index("head") * own_cols
    own_grad = lax.psum_scatter(
        grad_normed.astype(jnp.bfloat16), "head", scatter_dimension=1, tiled=True
    ).astype(jnp.float32)
    norm_own = lax.dynamic_slice_in_dim(norm32, start, own_cols, 1)
    spread_own = lax.dynamic_slice_in_dim(inv_spread, start, own_cols, 1)
    first = jnp.mean(own_grad, axis=-1, keepdims=True)
    second = jnp.mean(own_grad * norm_own, axis=-1, keepdims=True)
    d_input = spread_own * (own_grad - first - norm_own * second)
    grad_x = (grad_y.astype(jnp.float32) + d_input).astype(jnp.bfloat16)
    return (mixed, grad_x, grad_qkv_sum.astype(jnp.bfloat16), grad_out_sum.astype(jnp.bfloat16))


def solution(mesh):
    return jax.shard_map(
        on_device,
        mesh=mesh,
        in_specs=(
            P("lat", ("lon", "head"), None),
            P(None, "head", None),
            P("head", None),
            P("lat", "lon"),
            P("lat", ("lon", "head"), None),
        ),
        out_specs=(
            P("lat", ("lon", "head"), None),
            P("lat", ("lon", "head"), None),
            P(None, "head", None),
            P("head", None),
        ),
        check_vma=False,
    )
```

profile of v0, /device:TPU:22, one launch (start us, length us, event | category | flops | bytes accessed | tf_op | source)
XLA Modules:
  0.0 801.7 jit_solution(6272275382911569863)
XLA Ops:
  7.2 13.3 %all_gather.6 = bf16[8,32,768]{2,1,0:T(8,128)(2,1)S(1)} all-gather(bf16[8,8,768]{2,1,0:T(8,128)(2,1)} %param.11), channel_id=1, replica_groups=mesh['lat'=4,'lon'=32,'head'=4] {'head'}, dimensions={1}, use_global_device_ids=true | all-gather | bytes 491520 | tf_op jit(solution)/shard_map/all_gather | solution.py:79
  20.9 1.1 fusion.43
  23.2 1.9 collective-permute-start
  26.1 3.6 collective-permute-start.1
  30.4 1.9 collective-permute-start.4
  32.3 3.6 collective-permute-start.5
  36.0 12.9 %all_gather.7 = bf16[8,32,768]{2,1,0:T(8,128)(2,1)S(1)} all-gather(bf16[8,8,768]{2,1,0:T(8,128)(2,1)S(1)} %copy-done.30), channel_id=1, replica_groups=mesh['lat'=4,'lon'=32,'head'=4] {'head'}, dimensions={1}, use_global_device_ids=true | all-gather | bytes 491520 | tf_op jit(solution)/shard_map/all_gather | solution.py:145
  49.4 1.9 collective-permute-start.8
  53.0 3.8 collective-permute-start.6
  57.1 9.2 %collective-permute-start.7 = (bf16[20,6]{1,0:T(8,128)(2,1)S(1)}, bf16[20,6]{1,0:T(8,128)(2,1)S(1)}, u32[]{:S(2)}, u32[]{:S(2)}) collective-permute-start(bf16[20,6]{1,0:T(8,128)(2,1)S(1)} %get-tuple-element.559), channel_id=1, source_target_pairs={{4,0},{8,4},{12,8},{16,12},{20,16},{24,20},{28,24},{32,28},{36,32}... | collective-permute-start | bytes 728 | tf_op jit(solution)/shard_map/ppermute | solution.py:25
  66.6 4.0 collective-permute-start.9
  70.8 1.9 collective-permute-start.2
  72.7 7.5 collective-permute-start.3
  81.1 1.9 collective-permute-start.10
  83.0 7.7 collective-permute-start.11
  91.3 21.5 %while.28 = (s32[]{:T(128)}, bf16[2,128,192]{1,2,0:T(8,128)(2,1)}, f32[2,128,3]{1,0,2:T(2,128)S(1)}, s32[2]{0:T(128)S(1)}, bf16[20,44,192]{2,1,0:T(8,128)(2,1)S(...) while((s32[]{:T(128)}, bf16[2,128,192]{1,2,0:T(8,128)(2,1)}, ...), condition=%wide.region_5.6_spmd.clone, body=%wide.region_2.5_spmd.sunk.clone.sunk | while | flops 57153728 | bytes 6362401 | solution.py:134
  97.2 1.5 fusion.109
  100.0 1.4 convolution_convert_fusion.6
  107.9 1.5 fusion.109
  110.7 1.4 convolution_convert_fusion.6
  114.0 1.3 fusion.47
  117.6 1.9 collective-permute-start.12
  119.5 3.8 collective-permute-start.13
  123.3 1.3 pad_maximum_fusion.2
  124.6 1.1 fusion.59
  125.8 1.1 fusion.74
  127.7 1.9 collective-permute-start.14
  129.6 7.5 collective-permute-start.15
  141.8 46.7 %while.29 = (s32[]{:T(128)}, bf16[2,128,576]{1,2,0:T(8,128)(2,1)}, s32[2]{0:T(128)}, bf16[20,44,192]{2,1,0:T(8,128)(2,1)S(1)}, f32[20,44]{1,0:T(8,128)S(1)}, /*i...) while((s32[]{:T(128)}, bf16[2,128,576]{1,2,0:T(8,128)(2,1)}, ...), condition=%wide.region_8.9_spmd.clone, body=%wide.region_7.8_spmd.sunk.clone.sunk | while | flops 196101376 | bytes 18631896 | solution.py:226
  141.8 1.2 dynamic_slice.237
  145.6 1.4 constant_dynamic-slice_fusion.30
  147.1 1.3 convolution_subtract_fusion.3
  150.2 1.1 or_and_fusion.5
  152.1 2.4 fusion.125
  154.5 1.1 constant_dynamic-slice_fusion.26
  158.8 1.5 reshape.329
  162.5 1.6 fusion.124
  165.1 1.2 dynamic_slice.237
  168.9 1.4 constant_dynamic-slice_fusion.30
  170.4 1.3 convolution_subtract_fusion.3
  173.6 1.1 or_and_fusion.5
  175.5 2.4 fusion.125
  177.9 1.1 constant_dynamic-slice_fusion.26
  182.2 1.5 reshape.329
  185.9 1.6 fusion.124
  188.5 1.2 copy.100
  189.9 1.7 fusion.48
  193.1 598.3 %all-reduce.2 = (bf16[3,192,768]{2,1,0:T(8,128)(2,1)}, bf16[192,768]{1,0:T(8,128)(2,1)}) all-reduce(f32[3,192,768]{2,1,0:T(8,128)} %fusion.48, f32[192,768]{1,0:T(8,128)S(1)} %copy-done.15), channel_id=1, replica_groups=mesh['lat'=4,'lon'=32,'head'=4] {'lat','lon'}, use_global_device_ids=true, to_apply=%region_12.13 | all-reduce | flops 589824 | bytes 3538944 | tf_op jit(solution)/shard_map/psum | solution.py:231
  (282 shorter events, 50.5 us)
Async XLA Ops:
  7.2 14.9 %copy-start = (bf16[3,192,768]{2,1,0:T(8,128)(2,1)S(1)}, bf16[3,192,768]{2,1,0:T(8,128)(2,1)}, u32[]{:S(2)}) copy-start(bf16[3,192,768]{2,1,0:T(8,128)(2,1)} %param.12) | copy-start | bytes 2654212
  7.2 784.2 %reduce-scatter.7.cloned.1.call-start = ((), (), s32[]{:S(2)}) async-start(), calls=%async_computation.2 | async-start | bytes 491520
  22.5 7.3 copy-start.36
  22.5 13.5 %copy-start.30 = (bf16[8,8,768]{2,1,0:T(8,128)(2,1)S(1)}, bf16[8,8,768]{2,1,0:T(8,128)(2,1)}, u32[]{:S(2)}) copy-start(bf16[8,8,768]{2,1,0:T(8,128)(2,1)} %param.15) | copy-start | bytes 294916
  22.7 26.2 %copy-start.23 = (bf16[192,768]{1,0:T(8,128)(2,1)S(1)}, bf16[192,768]{1,0:T(8,128)(2,1)}, u32[]{:S(2)}) copy-start(bf16[192,768]{1,0:T(8,128)(2,1)} %param.13) | copy-start | bytes 884740
  23.2 47.4 %collective-permute-start = (bf16[6,32,384]{2,1,0:T(8,128)(2,1)S(1)}, bf16[6,32,384]{2,1,0:T(8,128)(2,1)S(1)}, u32[]{:S(2)}, u32[]{:S(2)}) collective-permute-start(bf16[6,32,384]{2,1,0:T(8,128)(2,1)S(1)} %slice.81), channel_id=1, source_target_pairs={{0,128},{128,256},{256,384},{384,0},{1,129},{129,257},{257,385},{3... | collective-permute-start | bytes 442376 | tf_op jit(solution)/shard_map/ppermute | solution.py:23
  26.1 44.6 %collective-permute-start.1 = (bf16[6,32,384]{2,1,0:T(8,128)(2,1)}, bf16[6,32,384]{2,1,0:T(8,128)(2,1)S(1)}, u32[]{:S(2)}, u32[]{:S(2)}) collective-permute-start(bf16[6,32,384]{2,1,0:T(8,128)(2,1)} %slice.84), channel_id=1, source_target_pairs={{128,0},{256,128},{384,256},{0,384},{129,1},{257,129},{385,257},{1... | collective-permute-start | bytes 442376 | tf_op jit(solution)/shard_map/ppermute | solution.py:25
  30.4 22.5 %collective-permute-start.4 = (bf16[6,32]{1,0:T(8,128)(2,1)S(1)}, bf16[6,32]{1,0:T(8,128)(2,1)S(1)}, u32[]{:S(2)}, u32[]{:S(2)}) collective-permute-start(bf16[6,32]{1,0:T(8,128)(2,1)S(1)} %get-tuple-element.562), channel_id=1, source_target_pairs={{0,128},{128,256},{256,384},{384,0},{1,129},{129,257},{257,385},{3... | collective-permute-start | bytes 1160 | tf_op jit(solution)/shard_map/ppermute | solution.py:23
  32.3 20.6 %collective-permute-start.5 = (bf16[6,32]{1,0:T(8,128)(2,1)S(1)}, bf16[6,32]{1,0:T(8,128)(2,1)S(1)}, u32[]{:S(2)}, u32[]{:S(2)}) collective-permute-start(bf16[6,32]{1,0:T(8,128)(2,1)S(1)} %get-tuple-element.563), channel_id=1, source_target_pairs={{128,0},{256,128},{384,256},{0,384},{129,1},{257,129},{385,257},{1... | collective-permute-start | bytes 1160 | tf_op jit(solution)/shard_map/ppermute | solution.py:25
  48.9 8.2 %copy-start.13 = (bf16[8,32,768]{2,1,0:T(8,128)(2,1)}, bf16[8,32,768]{2,1,0:T(8,128)(2,1)S(1)}, u32[]{:S(2)}) copy-start(bf16[8,32,768]{2,1,0:T(8,128)(2,1)S(1)} %all_gather.7) | copy-start | bytes 1179652
  49.4 30.8 %collective-permute-start.8 = (bf16[6,32,384]{2,1,0:T(8,128)(2,1)S(1)}, bf16[6,32,384]{2,1,0:T(8,128)(2,1)S(1)}, u32[]{:S(2)}, u32[]{:S(2)}) collective-permute-start(bf16[6,32,384]{2,1,0:T(8,128)(2,1)S(1)} %get-tuple-element.550), channel_id=1, source_target_pairs={{0,128},{128,256},{256,384},{384,0},{1,129},{129,257},{257,385},{3... | collective-permute-start | bytes 442376 | tf_op jit(solution)/shard_map/ppermute | solution.py:23
  51.4 19.4 %copy-start.37 = (f32[20]{0:T(128)}, f32[20]{0:T(128)S(1)}, u32[]{:S(2)}) copy-start(f32[20]{0:T(128)S(1)} %and_convert_fusion) | copy-start | bytes 244
  53.0 13.5 %collective-permute-start.6 = (bf16[20,6]{1,0:T(8,128)(2,1)S(1)}, bf16[20,6]{1,0:T(8,128)(2,1)S(1)}, u32[]{:S(2)}, u32[]{:S(2)}) collective-permute-start(bf16[20,6]{1,0:T(8,128)(2,1)S(1)} %get-tuple-element.558), channel_id=1, source_target_pairs={{0,4},{4,8},{8,12},{12,16},{16,20},{20,24},{24,28},{28,32},{32,36}... | collective-permute-start | bytes 728 | tf_op jit(solution)/shard_map/ppermute | solution.py:23
  57.1 13.4 %collective-permute-start.7 = (bf16[20,6]{1,0:T(8,128)(2,1)S(1)}, bf16[20,6]{1,0:T(8,128)(2,1)S(1)}, u32[]{:S(2)}, u32[]{:S(2)}) collective-permute-start(bf16[20,6]{1,0:T(8,128)(2,1)S(1)} %get-tuple-element.559), channel_id=1, source_target_pairs={{4,0},{8,4},{12,8},{16,12},{20,16},{24,20},{28,24},{32,28},{36,32}... | collective-permute-start | bytes 728 | tf_op jit(solution)/shard_map/ppermute | solution.py:25
  66.6 13.7 %collective-permute-start.9 = (bf16[6,32,384]{2,1,0:T(8,128)(2,1)S(1)}, bf16[6,32,384]{2,1,0:T(8,128)(2,1)S(1)}, u32[]{:S(2)}, u32[]{:S(2)}) collective-permute-start(bf16[6,32,384]{2,1,0:T(8,128)(2,1)S(1)} %get-tuple-element.551), channel_id=1, source_target_pairs={{128,0},{256,128},{384,256},{0,384},{129,1},{257,129},{385,257},{1... | collective-permute-start | bytes 442376 | tf_op jit(solution)/shard_map/ppermute | solution.py:25
  70.8 19.9 %collective-permute-start.2 = (bf16[20,6,384]{2,1,0:T(8,128)(2,1)S(1)}, bf16[20,6,384]{2,1,0:T(8,128)(2,1)S(1)}, u32[]{:S(2)}, u32[]{:S(2)}) collective-permute-start(bf16[20,6,384]{2,1,0:T(8,128)(2,1)S(1)} %get-tuple-element.544), channel_id=1, source_target_pairs={{0,4},{4,8},{8,12},{12,16},{16,20},{20,24},{24,28},{28,32},{32,36}... | collective-permute-start | bytes 276488 | tf_op jit(solution)/shard_map/ppermute | solution.py:23
  72.7 18.0 %collective-permute-start.3 = (bf16[20,6,384]{2,1,0:T(8,128)(2,1)S(1)}, bf16[20,6,384]{2,1,0:T(8,128)(2,1)S(1)}, u32[]{:S(2)}, u32[]{:S(2)}) collective-permute-start(bf16[20,6,384]{2,1,0:T(8,128)(2,1)S(1)} %get-tuple-element.545), channel_id=1, source_target_pairs={{4,0},{8,4},{12,8},{16,12},{20,16},{24,20},{28,24},{32,28},{36,32}... | collective-permute-start | bytes 276488 | tf_op jit(solution)/shard_map/ppermute | solution.py:25
  80.3 10.4 %copy-start.27 = (bf16[6,32,384]{2,1,0:T(8,128)(2,1)}, bf16[6,32,384]{2,1,0:T(8,128)(2,1)S(1)}, u32[]{:S(2)}) copy-start(bf16[6,32,384]{2,1,0:T(8,128)(2,1)S(1)} %collective-permute-done.9) | copy-start | bytes 442372
  81.1 42.2 %collective-permute-start.10 = (bf16[20,6,384]{2,1,0:T(8,128)(2,1)}, bf16[20,6,384]{2,1,0:T(8,128)(2,1)}, u32[]{:S(2)}, u32[]{:S(2)}) collective-permute-start(bf16[20,6,384]{2,1,0:T(8,128)(2,1)} %get-tuple-element.542), channel_id=1, source_target_pairs={{0,4},{4,8},{8,12},{12,16},{16,20},{20,24},{24,28},{28,32},{32,36}... | collective-permute-start | bytes 276488 | tf_op jit(solution)/shard_map/ppermute | solution.py:23
  83.0 8.3 %copy-start.8 = (pred[128,560]{0,1:T(8,128)(4,1)S(1)}, pred[128,560]{0,1:T(8,128)(4,1)}, u32[]{:S(2)}) copy-start(pred[128,560]{0,1:T(8,128)(4,1)} %constant.242.clone..sunk.4) | copy-start | bytes 215044
  83.0 40.3 %collective-permute-start.11 = (bf16[20,6,384]{2,1,0:T(8,128)(2,1)}, bf16[20,6,384]{2,1,0:T(8,128)(2,1)}, u32[]{:S(2)}, u32[]{:S(2)}) collective-permute-start(bf16[20,6,384]{2,1,0:T(8,128)(2,1)} %get-tuple-element.543), channel_id=1, source_target_pairs={{4,0},{8,4},{12,8},{16,12},{20,16},{24,20},{28,24},{32,28},{36,32}... | collective-permute-start | bytes 276488 | tf_op jit(solution)/shard_map/ppermute | solution.py:25
  112.8 10.5 %copy-start.26 = (bf16[6,32,384]{2,1,0:T(8,128)(2,1)S(1)}, bf16[6,32,384]{2,1,0:T(8,128)(2,1)}, u32[]{:S(2)}) copy-start(bf16[6,32,384]{2,1,0:T(8,128)(2,1)} %copy-done.25) | copy-start | bytes 442372
  112.8 10.5 %copy-start.28 = (bf16[6,32,384]{2,1,0:T(8,128)(2,1)S(1)}, bf16[6,32,384]{2,1,0:T(8,128)(2,1)}, u32[]{:S(2)}) copy-start(bf16[6,32,384]{2,1,0:T(8,128)(2,1)} %copy-done.27) | copy-start | bytes 442372
  117.6 9.3 %collective-permute-start.12 = (f32[6,32,6]{1,0,2:T(8,128)S(1)}, f32[6,32,6]{1,0,2:T(8,128)S(1)}, u32[]{:S(2)}, u32[]{:S(2)}) collective-permute-start(f32[6,32,6]{1,0,2:T(8,128)S(1)} %get-tuple-element.556), channel_id=1, source_target_pairs={{0,128},{128,256},{256,384},{384,0},{1,129},{129,257},{257,385},{3... | collective-permute-start | bytes 13832 | tf_op jit(solution)/shard_map/ppermute | solution.py:23
  119.5 6.3 copy-start.14
  119.5 7.3 collective-permute-start.13
  124.6 12.6 %copy-start.24 = (bf16[192,768]{1,0:T(8,128)(2,1)S(1)}, bf16[192,768]{1,0:T(8,128)(2,1)}, u32[]{:S(2)}) copy-start(bf16[192,768]{1,0:T(8,128)(2,1)} %param.13) | copy-start | bytes 884740
  126.8 13.7 %copy-start.38 = (f32[20]{0:T(128)S(1)}, f32[20]{0:T(128)}, u32[]{:S(2)}) copy-start(f32[20]{0:T(128)} %copy-done.37) | copy-start | bytes 244
  127.7 10.8 %collective-permute-start.14 = (f32[20,6,6]{1,0,2:T(8,128)S(1)}, f32[20,6,6]{1,0,2:T(8,128)S(1)}, u32[]{:S(2)}, u32[]{:S(2)}) collective-permute-start(f32[20,6,6]{1,0,2:T(8,128)S(1)} %get-tuple-element.554), channel_id=1, source_target_pairs={{0,4},{4,8},{8,12},{12,16},{16,20},{20,24},{24,28},{28,32},{32,36}... | collective-permute-start | bytes 8648 | tf_op jit(solution)/shard_map/ppermute | solution.py:23
  129.6 9.5 %collective-permute-start.15 = (f32[20,6,6]{1,0,2:T(8,128)S(1)}, f32[20,6,6]{1,0,2:T(8,128)S(1)}, u32[]{:S(2)}, u32[]{:S(2)}) collective-permute-start(f32[20,6,6]{1,0,2:T(8,128)S(1)} %get-tuple-element.555), channel_id=1, source_target_pairs={{4,0},{8,4},{12,8},{16,12},{20,16},{24,20},{28,24},{32,28},{36,32}... | collective-permute-start | bytes 8648 | tf_op jit(solution)/shard_map/ppermute | solution.py:25
  138.2 654.8 %reduce-scatter.9.cloned.1.call-start = ((), (), s32[]{:S(2)}) async-start(), calls=%async_computation.3 | async-start | bytes 491520
  141.8 6.6 copy-start.2
  141.8 6.6 copy-start.6
  141.8 7.5 copy-start.17
  141.8 8.5 %copy-start.9 = (pred[128,560]{0,1:T(8,128)(4,1)}, pred[128,560]{0,1:T(8,128)(4,1)S(1)}, u32[]{:S(2)}) copy-start(pred[128,560]{0,1:T(8,128)(4,1)S(1)} %get-tuple-element.879) | copy-start | bytes 215044 | tf_op jit(solution)/shard_map/while
  141.8 15.8 %copy-start.19 = (f32[20,44,3]{1,0,2:T(8,128)}, f32[20,44,3]{1,0,2:T(8,128)S(1)}, u32[]{:S(2)}) copy-start(f32[20,44,3]{1,0,2:T(8,128)S(1)} %get-tuple-element.873) | copy-start | bytes 31684 | tf_op jit(solution)/shard_map/while
  148.9 5.6 copy-start.4
  148.9 5.6 copy-start.5
  165.1 6.6 copy-start.2
  165.1 6.6 copy-start.6
  165.1 7.5 copy-start.17
  165.1 8.5 %copy-start.9 = (pred[128,560]{0,1:T(8,128)(4,1)}, pred[128,560]{0,1:T(8,128)(4,1)S(1)}, u32[]{:S(2)}) copy-start(pred[128,560]{0,1:T(8,128)(4,1)S(1)} %get-tuple-element.879) | copy-start | bytes 215044 | tf_op jit(solution)/shard_map/while
  165.1 15.8 %copy-start.19 = (f32[20,44,3]{1,0,2:T(8,128)}, f32[20,44,3]{1,0,2:T(8,128)S(1)}, u32[]{:S(2)}) copy-start(f32[20,44,3]{1,0,2:T(8,128)S(1)} %get-tuple-element.873) | copy-start | bytes 31684 | tf_op jit(solution)/shard_map/while
  172.3 5.6 copy-start.4
  193.0 599.3 %copy-start.29 = (bf16[8,8,768]{2,1,0:T(8,128)(2,1)S(1)}, bf16[8,8,768]{2,1,0:T(8,128)(2,1)}, u32[]{:S(2)}) copy-start(bf16[8,8,768]{2,1,0:T(8,128)(2,1)} %param.11) | copy-start | bytes 294916
  193.1 600.9 %copy-start.16 = (f32[8,32,768]{2,1,0:T(8,128)S(1)}, f32[8,32,768]{2,1,0:T(8,128)}, u32[]{:S(2)}) copy-start(f32[8,32,768]{2,1,0:T(8,128)} %get-tuple-element.546) | copy-start | bytes 2359300
  193.1 601.0 %copy-start.31 = (bf16[8,8,768]{2,1,0:T(8,128)(2,1)S(1)}, bf16[8,8,768]{2,1,0:T(8,128)(2,1)}, u32[]{:S(2)}) copy-start(bf16[8,8,768]{2,1,0:T(8,128)(2,1)} %param.15) | copy-start | bytes 294916
  193.1 601.0 %copy-start.35 = (f32[8,8]{1,0:T(8,128)S(1)}, f32[8,8]{1,0:T(8,128)}, u32[]{:S(2)}) copy-start(f32[8,8]{1,0:T(8,128)} %constant_dynamic-slice_fusion.15) | copy-start | bytes 772
  (27 other events, 61.3 us)
Sparse Core Ops, SparseCore 0:
  138.3 17.3 reduce-scatter.6
  193.2 22.4 reduce-scatter.8
where the time goes:
time: 804 us; the launch traced here: 802 us
  blocking collectives  625 us (78%)
  starting transfers between devices  64.5 us (8%)
  local copies, waits for them, and re-layouts  48.8 us (6%)
  matrix products  22 us (3%)
  other arithmetic  16.5 us (2%)
  between operations  14.8 us (2%)
  loops' own time  9.79 us (1%)
    psum x1, blocking collectives, on_device(): lax.psum((grad_qkv_local, grad_out_local), ('lat', 'lon'))  598 us
    ppermute x8, starting transfers between devices, extended(): lax.ppermute(head, axis, [((i + 1) % count, i) for i in range(count)])  47 us
    ppermute x8, starting transfers between devices, extended(): lax.ppermute(tail, axis, [(i, (i + 1) % count) for i in range(count)])  17.2 us
  transfers between devices with their start and end apart: 18, of which 1 were waited for; matrix products, arithmetic and copies ran while one was open for 10% of the time, Pallas kernels for 0%

commit v1 on v0

--- a/solution.py
+++ b/solution.py
@@ -1,8 +1,266 @@
+import functools
+
 import jax
 import jax.numpy as jnp
 import numpy as np
 from jax import lax
+from jax.experimental import pallas as pl
+from jax.experimental.pallas import tpu as pltpu
 from jax.sharding import PartitionSpec as P
+
+MESH = pl.DeviceIdType.MESH
+N_Z = 16
+N_Y = 4
+N_OWN = 9
+
+
+class Place:
+    def __init__(self):
+        self.lat = lax.axis_index("lat")
+        self.lon = lax.axis_index("lon")
+        self.head = lax.axis_index("head")
+        self.core = lax.rem(self.lat, 2)
+        self.y = (self.lon // N_Z) * 2 + self.lat // 2
+        self.z = lax.rem(self.lon, N_Z)
+
+    def at(self, core=None, y=None, z=None):
+        core = self.core if core is None else core
+        y = self.y if y is None else y
+        z = self.z if z is None else z
+        return (lax.rem(y, 2) * 2 + core, (y // 2) * N_Z + z, self.head)
+
+
+def remote(src, dst, send_sem, recv_sem, device):
+    return pltpu.make_async_remote_copy(
+        src_ref=src,
+        dst_ref=dst,
+        send_sem=send_sem,
+        recv_sem=recv_sem,
+        device_id=device,
+        device_id_type=MESH,
+    )
+
+
+class Summed:
+    def __init__(self, place, turn, src, res, cbuf, ybuf, zbuf, sem_c, sem_y, sem_z, sem_zg, sem_yg, sem_cg):
+        self.p = place
+        self.src, self.res, self.cbuf, self.ybuf, self.zbuf = src, res, cbuf, ybuf, zbuf
+        self.sem_c, self.sem_y, self.sem_z = sem_c, sem_y, sem_z
+        self.sem_zg, self.sem_yg, self.sem_cg = sem_zg, sem_yg, sem_cg
+        self.turn = turn
+        turned = lax.rem(place.z + N_Z - turn, N_Z)
+        self.mine = (turned * N_OWN + N_Z - 1) // N_Z
+        self.owner = (self.mine * N_Z) // N_OWN == turned
+        self.mine = jnp.minimum(self.mine, N_OWN - 1)
+
+    @staticmethod
+    def scratch(t):
+        bf = jnp.bfloat16
+        return [
+            pltpu.VMEM((2, N_Y, N_OWN, t, 128), bf),
+            pltpu.VMEM((2, N_Y, N_OWN, t, 128), bf),
+            pltpu.VMEM((N_Y, N_OWN, t, 128), bf),
+            pltpu.VMEM((N_Y, N_OWN, t, 128), bf),
+            pltpu.VMEM((N_Z, t, 128), bf),
+            pltpu.SemaphoreType.DMA((2,)),
+            pltpu.SemaphoreType.DMA((2, N_Y)),
+            pltpu.SemaphoreType.DMA((2, N_Z)),
+            pltpu.SemaphoreType.DMA((2, N_Z)),
+            pltpu.SemaphoreType.DMA((2, N_Y)),
+            pltpu.SemaphoreType.DMA((2, N_Y)),
+        ]
+
+    def core_copy(self):
+        p = self.p
+        return remote(
+            self.src.at[1 - p.core], self.cbuf, self.sem_c.at[0], self.sem_c.at[1], p.at(core=1 - p.core)
+        )
+
+    def y_copy(self, step, arriving=False):
+        p = self.p
+        y = lax.rem(p.y + step, N_Y)
+        slot = y if arriving else p.y
+        return remote(
+            self.src.at[p.core, y], self.ybuf.at[slot], self.sem_y.at[0, y], self.sem_y.at[1, slot], p.at(y=y)
+        )
+
+    def owner_z(self, tile):
+        return lax.rem((tile * N_Z) // N_OWN + self.turn, N_Z)
+
+    def z_copy(self, tile):
+        p = self.p
+        return remote(
+            self.src.at[p.core, p.y, tile],
+            self.zbuf.at[p.z],
+            self.sem_z.at[0, tile],
+            self.sem_z.at[1, p.z],
+            p.at(z=self.owner_z(tile)),
+        )
+
+    def z_arrival(self, z):
+        p = self.p
+        return remote(
+            self.src.at[p.core, p.y, 0], self.zbuf.at[z], self.sem_z.at[0, 0], self.sem_z.at[1, z], p.at(z=z)
+        )
+
+    def zg_copy(self, z, tile):
+        p = self.p
+        here = self.res.at[p.core, p.y, tile]
+        return remote(here, here, self.sem_zg.at[0, z], self.sem_zg.at[1, tile], p.at(z=z))
+
+    def yg_copy(self, step, arriving=False):
+        p = self.p
+        y = lax.rem(p.y + step, N_Y)
+        slot = y if arriving else p.y
+        here = self.res.at[p.core, slot]
+        return remote(here, here, self.sem_yg.at[0, y], self.sem_yg.at[1, slot], p.at(y=y))
+
+    def cg_copy(self, y, arriving=False):
+        p = self.p
+        here = self.res.at[1 - p.core if arriving else p.core, y]
+        return remote(here, here, self.sem_cg.at[0, y], self.sem_cg.at[1, y], p.at(core=1 - p.core))
+
+    def send_core(self):
+        self.core_copy().start()
+
+    def core_to_y(self):
+        p = self.p
+        self.core_copy().wait_recv()
+        for step in (2, 1, 3, 0):
+            y = lax.rem(p.y + step, N_Y)
+            both = self.src[p.core, y].astype(jnp.float32) + self.cbuf[y].astype(jnp.float32)
+            self.src[p.core, y] = both.astype(jnp.bfloat16)
+            if step:
+                self.y_copy(step).start()
+
+    def y_to_z(self):
+        p = self.p
+        for step in (1, 3, 2):
+            self.y_copy(step, True).wait_recv()
+        total = self.src[p.core, p.y].astype(jnp.float32)
+        for step in (1, 2, 3):
+            total = total + self.ybuf[lax.rem(p.y + step, N_Y)].astype(jnp.float32)
+        self.src[p.core, p.y] = total.astype(jnp.bfloat16)
+
+        @pl.loop(0, N_OWN)
+        def _(tile):
+            @pl.when(self.owner_z(tile) != p.z)
+            def _():
+                self.z_copy(tile).start()
+
+    def z_to_all(self):
+        p = self.p
+
+        @pl.when(self.owner)
+        def _():
+            @pl.loop(1, N_Z)
+            def _(step):
+                self.z_arrival(lax.rem(p.z + step, N_Z)).wait_recv()
+
+            def add(step, total):
+                return total + self.zbuf[lax.rem(p.z + step, N_Z)].astype(jnp.float32)
+
+            own = self.src[p.core, p.y, self.mine].astype(jnp.float32)
+            total = lax.fori_loop(1, N_Z, add, own)
+            self.res[p.core, p.y, self.mine] = total.astype(jnp.bfloat16)
+
+            @pl.loop(1, N_Z)
+            def _(step):
+                self.zg_copy(lax.rem(p.z + step, N_Z), self.mine).start()
+
+    def all_to_y(self):
+        p = self.p
+
+        @pl.loop(0, N_OWN)
+        def _(tile):
+            @pl.when(self.owner_z(tile) != p.z)
+            def _():
+                self.zg_copy(0, tile).wait_recv()
+
+        for step in (2, 1, 3):
+            self.yg_copy(step).start()
+        self.cg_copy(p.y).start()
+
+    def y_to_core(self):
+        p = self.p
+        for step in (1, 3, 2):
+            self.yg_copy(step, True).wait_recv()
+            self.cg_copy(lax.rem(p.y + step, N_Y)).start()
+
+    def finish(self):
+        p = self.p
+        for y in range(N_Y):
+            self.cg_copy(y, True).wait_recv()
+        self.core_copy().wait_send()
+        for step in (1, 2, 3):
+            self.y_copy(step).wait_send()
+            self.yg_copy(step).wait_send()
+        for y in range(N_Y):
+            self.cg_copy(y).wait_send()
+
+        @pl.loop(0, N_OWN)
+        def _(tile):
+            @pl.when(self.owner_z(tile) != p.z)
+            def _():
+                self.z_copy(tile).wait_send()
+
+        @pl.when(self.owner)
+        def _():
+            @pl.loop(1, N_Z)
+            def _(step):
+                self.zg_copy(lax.rem(p.z + step, N_Z), self.mine).wait_send()
+
+
+def sum_kernel(t, part_ref, out_ref, *scratch):
+    place = Place()
+    barrier = pltpu.get_barrier_semaphore()
+    pl.semaphore_signal(barrier, inc=1, device_id=place.at(core=1 - place.core), device_id_type=MESH)
+    for step in range(1, N_Y):
+        pl.semaphore_signal(
+            barrier, inc=1, device_id=place.at(y=lax.rem(place.y + step, N_Y)), device_id_type=MESH
+        )
+
+    @pl.loop(1, N_Z)
+    def _(step):
+        pl.semaphore_signal(
+            barrier, inc=1, device_id=place.at(z=lax.rem(place.z + step, N_Z)), device_id_type=MESH
+        )
+
+    summed = Summed(place, 0, *scratch)
+    for core in range(2):
+        for y in range(N_Y):
+            for tile in range(N_OWN):
+                top = y * 3 * t + tile // 3 * t
+                left = core * 384 + tile % 3 * 128
+                summed.src[core, y, tile] = part_ref[top : top + t, left : left + 128].astype(jnp.bfloat16)
+    pl.semaphore_wait(barrier, 1 + N_Y - 1 + N_Z - 1)
+    summed.send_core()
+    summed.core_to_y()
+    summed.y_to_z()
+    summed.z_to_all()
+    summed.all_to_y()
+    summed.y_to_core()
+    summed.finish()
+    for core in range(2):
+        for y in range(N_Y):
+            for tile in range(N_OWN):
+                top = y * 3 * t + tile // 3 * t
+                left = core * 384 + tile % 3 * 128
+                out_ref[top : top + t, left : left + 128] = summed.res[core, y, tile]
+
+
+def summed_over_cells(part):
+    t = part.shape[0] // 12
+    return pl.pallas_call(
+        functools.partial(sum_kernel, t),
+        out_shape=jax.ShapeDtypeStruct(part.shape, jnp.bfloat16),
+        in_specs=[pl.BlockSpec(memory_space=pltpu.VMEM)],
+        out_specs=pl.BlockSpec(memory_space=pltpu.VMEM),
+        scratch_shapes=Summed.scratch(t),
+        compiler_params=pltpu.CompilerParams(
+            collective_id=0, has_side_effects=True, vmem_limit_bytes=40 * 2**20
+        ),
+    )(part)
 
 HEAD_SIZE = 64
 REACH = 6
@@ -228,7 +486,8 @@
     grad_qkv_local = jnp.einsum(
         "nkc,nd->kcd", grad_projected, normed.reshape(-1, full), preferred_element_type=jnp.float32
     )
-    grad_qkv_sum, grad_out_sum = lax.psum((grad_qkv_local, grad_out_local), ("lat", "lon"))
+    parts = jnp.concatenate([grad_qkv_local.reshape(3 * width, full), grad_out_local], axis=0)
+    sums = summed_over_cells(parts)
     grad_normed = jnp.einsum(
         "nkc,kcd->nd", grad_projected, qkv_weight, preferred_element_type=jnp.float32
     )
@@ -243,7 +502,7 @@
     second = jnp.mean(own_grad * norm_own, axis=-1, keepdims=True)
     d_input = spread_own * (own_grad - first - norm_own * second)
     grad_x = (grad_y.astype(jnp.float32) + d_input).astype(jnp.bfloat16)
-    return (mixed, grad_x, grad_qkv_sum.astype(jnp.bfloat16), grad_out_sum.astype(jnp.bfloat16))
+    return (mixed, grad_x, sums[: 3 * width].reshape(3, width, full), sums[3 * width :])
 
 
 def solution(mesh):

time: 804 us -> 261 us (0.32)
  the two profiles are of different devices: /device:TPU:22 before, /device:TPU:1 now
where the time goes in v1:
time: 261 us; the launch traced here: 260 us
  starting transfers between devices  71.7 us (27%)
  Pallas kernels  53 us (20%)
  local copies, waits for them, and re-layouts  50.9 us (20%)
  blocking collectives  20.8 us (8%)
  matrix products  19.9 us (8%)
  other arithmetic  16.7 us (6%)
  between operations  14.9 us (6%)
  loops' own time  10.3 us (4%)
    pallas_call x1, Pallas kernels, summed_over_cells(): pl.pallas_call(functools.partial(sum_kernel, t), out_shape=jax.ShapeDtype...  53 us
    ppermute x8, starting transfers between devices, extended(): lax.ppermute(head, axis, [((i + 1) % count, i) for i in range(count)])  45.2 us
    ppermute x8, starting transfers between devices, extended(): lax.ppermute(tail, axis, [(i, (i + 1) % count) for i in range(count)])  26.2 us
    reshape x28, local copies, waits for them, and re-layouts, by_heads(): return piece.reshape(piece.shape[0], heads, HEAD_SIZE)  14.2 us
    all_gather x1, blocking collectives, on_device(): whole = lax.all_gather(activations, 'head', axis=1, tiled=True)  11.2 us
    all_gather x1, blocking collectives, on_device(): grad_full = lax.all_gather(grad_y, 'head', axis=1, tiled=True)  9.63 us
    dynamic_slice x16, local copies, waits for them, and re-layouts, cut_block(): piece = lax.dynamic_slice(field, starts, (rows, cols) + field.shape[2:])  9.09 us
    another operation x1, loops' own time, on_device(): grad_tiles = lax.map(backward_tile, tile_ids)  6.26 us
  transfers between devices with their start and end apart: 18, of which 2 were waited for; matrix products, arithmetic and copies ran while one was open for 31% of the time, Pallas kernels for 20%

profile of v1, /device:TPU:1, one launch (start us, length us, event | category | flops | bytes accessed | tf_op | source)
XLA Modules:
  0.0 259.5 jit_solution(13088083004191221228)
XLA Ops:
  7.2 11.2 %all_gather.6 = bf16[8,32,768]{2,1,0:T(8,128)(2,1)S(1)} all-gather(bf16[8,8,768]{2,1,0:T(8,128)(2,1)} %param.11), channel_id=1, replica_groups=mesh['lat'=4,'lon'=32,'head'=4] {'head'}, dimensions={1}, use_global_device_ids=true | all-gather | bytes 491520 | tf_op jit(solution)/shard_map/all_gather | solution.py:337
  18.8 1.2 fusion.43
  21.1 6.7 %collective-permute-start = (bf16[6,32,384]{2,1,0:T(8,128)(2,1)S(1)}, bf16[6,32,384]{2,1,0:T(8,128)(2,1)S(1)}, u32[]{:S(2)}, u32[]{:S(2)}) collective-permute-start(bf16[6,32,384]{2,1,0:T(8,128)(2,1)S(1)} %slice.87), channel_id=1, source_target_pairs={{0,128},{128,256},{256,384},{384,0},{1,129},{129,257},{257,385},{3... | collective-permute-start | bytes 442376 | tf_op jit(solution)/shard_map/ppermute | solution.py:281
  28.7 5.8 %collective-permute-start.1 = (bf16[6,32,384]{2,1,0:T(8,128)(2,1)}, bf16[6,32,384]{2,1,0:T(8,128)(2,1)S(1)}, u32[]{:S(2)}, u32[]{:S(2)}) collective-permute-start(bf16[6,32,384]{2,1,0:T(8,128)(2,1)} %slice.90), channel_id=1, source_target_pairs={{128,0},{256,128},{384,256},{0,384},{129,1},{257,129},{385,257},{1... | collective-permute-start | bytes 442376 | tf_op jit(solution)/shard_map/ppermute | solution.py:283
  35.1 1.9 collective-permute-start.4
  37.0 3.6 %collective-permute-start.5 = (bf16[6,32]{1,0:T(8,128)(2,1)S(1)}, bf16[6,32]{1,0:T(8,128)(2,1)S(1)}, u32[]{:S(2)}, u32[]{:S(2)}) collective-permute-start(bf16[6,32]{1,0:T(8,128)(2,1)S(1)} %get-tuple-element.561), channel_id=1, source_target_pairs={{128,0},{256,128},{384,256},{0,384},{129,1},{257,129},{385,257},{1... | collective-permute-start | bytes 1160 | tf_op jit(solution)/shard_map/ppermute | solution.py:283
  40.7 9.6 %all_gather.7 = bf16[8,32,768]{2,1,0:T(8,128)(2,1)S(1)} all-gather(bf16[8,8,768]{2,1,0:T(8,128)(2,1)S(1)} %copy-done.31), channel_id=1, replica_groups=mesh['lat'=4,'lon'=32,'head'=4] {'head'}, dimensions={1}, use_global_device_ids=true | all-gather | bytes 491520 | tf_op jit(solution)/shard_map/all_gather | solution.py:403
  50.9 5.2 %collective-permute-start.8 = (bf16[6,32,384]{2,1,0:T(8,128)(2,1)S(1)}, bf16[6,32,384]{2,1,0:T(8,128)(2,1)S(1)}, u32[]{:S(2)}, u32[]{:S(2)}) collective-permute-start(bf16[6,32,384]{2,1,0:T(8,128)(2,1)S(1)} %get-tuple-element.548), channel_id=1, source_target_pairs={{0,128},{128,256},{256,384},{384,0},{1,129},{129,257},{257,385},{3... | collective-permute-start | bytes 442376 | tf_op jit(solution)/shard_map/ppermute | solution.py:281
  57.8 1.9 collective-permute-start.6
  60.0 10.9 %collective-permute-start.7 = (bf16[20,6]{1,0:T(8,128)(2,1)S(1)}, bf16[20,6]{1,0:T(8,128)(2,1)S(1)}, u32[]{:S(2)}, u32[]{:S(2)}) collective-permute-start(bf16[20,6]{1,0:T(8,128)(2,1)S(1)} %get-tuple-element.557), channel_id=1, source_target_pairs={{4,0},{8,4},{12,8},{16,12},{20,16},{24,20},{28,24},{32,28},{36,32}... | collective-permute-start | bytes 728 | tf_op jit(solution)/shard_map/ppermute | solution.py:283
  71.1 1.9 collective-permute-start.9
  73.3 1.9 collective-permute-start.2
  75.2 7.0 %collective-permute-start.3 = (bf16[20,6,384]{2,1,0:T(8,128)(2,1)S(1)}, bf16[20,6,384]{2,1,0:T(8,128)(2,1)S(1)}, u32[]{:S(2)}, u32[]{:S(2)}) collective-permute-start(bf16[20,6,384]{2,1,0:T(8,128)(2,1)S(1)} %get-tuple-element.543), channel_id=1, source_target_pairs={{4,0},{8,4},{12,8},{16,12},{20,16},{24,20},{28,24},{32,28},{36,32}... | collective-permute-start | bytes 276488 | tf_op jit(solution)/shard_map/ppermute | solution.py:283
  83.0 1.9 collective-permute-start.10
  85.0 7.1 %collective-permute-start.11 = (bf16[20,6,384]{2,1,0:T(8,128)(2,1)}, bf16[20,6,384]{2,1,0:T(8,128)(2,1)}, u32[]{:S(2)}, u32[]{:S(2)}) collective-permute-start(bf16[20,6,384]{2,1,0:T(8,128)(2,1)} %get-tuple-element.541), channel_id=1, source_target_pairs={{4,0},{8,4},{12,8},{16,12},{20,16},{24,20},{28,24},{32,28},{36,32}... | collective-permute-start | bytes 276488 | tf_op jit(solution)/shard_map/ppermute | solution.py:283
  92.7 21.5 %while.28 = (s32[]{:T(128)}, bf16[2,128,192]{1,2,0:T(8,128)(2,1)}, f32[2,128,3]{1,0,2:T(2,128)S(1)}, s32[2]{0:T(128)S(1)}, bf16[20,44,192]{2,1,0:T(8,128)(2,1)S(...) while((s32[]{:T(128)}, bf16[2,128,192]{1,2,0:T(8,128)(2,1)}, ...), condition=%wide.region_5.6_spmd.clone, body=%wide.region_2.5_spmd.sunk.clone.sunk | while | flops 57153728 | bytes 6362401 | solution.py:392
  97.6 1.0 or_and_fusion.4
  98.6 1.5 fusion.109
  101.3 1.4 convolution_convert_fusion.6
  109.3 1.5 fusion.109
  112.1 1.4 convolution_convert_fusion.6
  114.2 1.0 copy.91
  115.4 1.3 fusion.47
  119.0 4.8 %collective-permute-start.12 = (f32[6,32,6]{1,0,2:T(8,128)S(1)}, f32[6,32,6]{1,0,2:T(8,128)S(1)}, u32[]{:S(2)}, u32[]{:S(2)}) collective-permute-start(f32[6,32,6]{1,0,2:T(8,128)S(1)} %get-tuple-element.554), channel_id=1, source_target_pairs={{0,128},{128,256},{256,384},{384,0},{1,129},{129,257},{257,385},{3... | collective-permute-start | bytes 13832 | tf_op jit(solution)/shard_map/ppermute | solution.py:281
  123.8 1.9 collective-permute-start.13
  125.7 1.3 pad_maximum_fusion.3
  127.0 1.1 fusion.57
  129.7 1.9 collective-permute-start.14
  131.7 7.0 %collective-permute-start.15 = (f32[20,6,6]{1,0,2:T(8,128)S(1)}, f32[20,6,6]{1,0,2:T(8,128)S(1)}, u32[]{:S(2)}, u32[]{:S(2)}) collective-permute-start(f32[20,6,6]{1,0,2:T(8,128)S(1)} %get-tuple-element.553), channel_id=1, source_target_pairs={{4,0},{8,4},{12,8},{16,12},{20,16},{24,20},{28,24},{32,28},{36,32}... | collective-permute-start | bytes 8648 | tf_op jit(solution)/shard_map/ppermute | solution.py:283
  143.1 47.3 %while.29 = (s32[]{:T(128)}, bf16[2,128,576]{1,2,0:T(8,128)(2,1)}, s32[2]{0:T(128)}, bf16[20,44,192]{2,1,0:T(8,128)(2,1)S(1)}, f32[20,44]{1,0:T(8,128)S(1)}, /*i...) while((s32[]{:T(128)}, bf16[2,128,576]{1,2,0:T(8,128)(2,1)}, ...), condition=%wide.region_8.9_spmd.clone, body=%wide.region_7.8_spmd.sunk.clone.sunk | while | flops 196101376 | bytes 18631896 | solution.py:484
  143.1 1.3 dynamic_slice.237
  147.2 1.4 constant_dynamic-slice_fusion.30
  148.7 1.3 convolution_subtract_fusion.3
  151.8 1.1 or_and_fusion.5
  153.7 2.4 fusion.125
  156.1 1.1 constant_dynamic-slice_fusion.26
  160.5 1.5 reshape.335
  164.2 1.6 fusion.124
  166.8 1.3 dynamic_slice.237
  170.9 1.4 constant_dynamic-slice_fusion.30
  172.4 1.3 convolution_subtract_fusion.3
  175.5 1.1 or_and_fusion.5
  177.4 2.4 fusion.125
  179.8 1.1 constant_dynamic-slice_fusion.26
  184.2 1.5 reshape.335
  187.9 1.6 fusion.124
  190.4 1.2 copy.98
  194.4 53.0 %shard_map.102 = bf16[768,768]{1,0:T(8,128)(2,1)S(1)} custom-call(f32[768,768]{1,0:T(8,128)S(1)} %pad_maximum_fusion.1.part_ref), custom_call_target="tpu_custom_call" | custom-call | tf_op jit(solution)/shard_map/pallas_call | solution.py:254
  (288 shorter events, 51.9 us)
Async XLA Ops:
  7.2 12.8 %copy-start = (bf16[3,192,768]{2,1,0:T(8,128)(2,1)S(1)}, bf16[3,192,768]{2,1,0:T(8,128)(2,1)}, u32[]{:S(2)}) copy-start(bf16[3,192,768]{2,1,0:T(8,128)(2,1)} %param.12) | copy-start | bytes 2654212
  7.2 242.0 %reduce-scatter.7.cloned.1.call-start = ((), (), s32[]{:S(2)}) async-start(), calls=%async_computation.2 | async-start | bytes 491520
  20.4 14.1 %copy-start.37 = (s32[8,32]{1,0:T(8,128)S(1)}, s32[8,32]{1,0:T(8,128)}, u32[]{:S(2)}) copy-start(s32[8,32]{1,0:T(8,128)} %param.14) | copy-start | bytes 3076
  20.4 20.3 %copy-start.31 = (bf16[8,8,768]{2,1,0:T(8,128)(2,1)S(1)}, bf16[8,8,768]{2,1,0:T(8,128)(2,1)}, u32[]{:S(2)}) copy-start(bf16[8,8,768]{2,1,0:T(8,128)(2,1)} %param.15) | copy-start | bytes 294916
  20.6 29.8 %copy-start.24 = (bf16[192,768]{1,0:T(8,128)(2,1)S(1)}, bf16[192,768]{1,0:T(8,128)(2,1)}, u32[]{:S(2)}) copy-start(bf16[192,768]{1,0:T(8,128)(2,1)} %param.13) | copy-start | bytes 884740
  21.1 52.1 %collective-permute-start = (bf16[6,32,384]{2,1,0:T(8,128)(2,1)S(1)}, bf16[6,32,384]{2,1,0:T(8,128)(2,1)S(1)}, u32[]{:S(2)}, u32[]{:S(2)}) collective-permute-start(bf16[6,32,384]{2,1,0:T(8,128)(2,1)S(1)} %slice.87), channel_id=1, source_target_pairs={{0,128},{128,256},{256,384},{384,0},{1,129},{129,257},{257,385},{3... | collective-permute-start | bytes 442376 | tf_op jit(solution)/shard_map/ppermute | solution.py:281
  28.7 44.5 %collective-permute-start.1 = (bf16[6,32,384]{2,1,0:T(8,128)(2,1)}, bf16[6,32,384]{2,1,0:T(8,128)(2,1)S(1)}, u32[]{:S(2)}, u32[]{:S(2)}) collective-permute-start(bf16[6,32,384]{2,1,0:T(8,128)(2,1)} %slice.90), channel_id=1, source_target_pairs={{128,0},{256,128},{384,256},{0,384},{129,1},{257,129},{385,257},{1... | collective-permute-start | bytes 442376 | tf_op jit(solution)/shard_map/ppermute | solution.py:283
  35.1 22.6 %collective-permute-start.4 = (bf16[6,32]{1,0:T(8,128)(2,1)S(1)}, bf16[6,32]{1,0:T(8,128)(2,1)S(1)}, u32[]{:S(2)}, u32[]{:S(2)}) collective-permute-start(bf16[6,32]{1,0:T(8,128)(2,1)S(1)} %get-tuple-element.560), channel_id=1, source_target_pairs={{0,128},{128,256},{256,384},{384,0},{1,129},{129,257},{257,385},{3... | collective-permute-start | bytes 1160 | tf_op jit(solution)/shard_map/ppermute | solution.py:281
  37.0 20.7 %collective-permute-start.5 = (bf16[6,32]{1,0:T(8,128)(2,1)S(1)}, bf16[6,32]{1,0:T(8,128)(2,1)S(1)}, u32[]{:S(2)}, u32[]{:S(2)}) collective-permute-start(bf16[6,32]{1,0:T(8,128)(2,1)S(1)} %get-tuple-element.561), channel_id=1, source_target_pairs={{128,0},{256,128},{384,256},{0,384},{129,1},{257,129},{385,257},{1... | collective-permute-start | bytes 1160 | tf_op jit(solution)/shard_map/ppermute | solution.py:283
  50.3 9.6 %copy-start.13 = (bf16[8,32,768]{2,1,0:T(8,128)(2,1)}, bf16[8,32,768]{2,1,0:T(8,128)(2,1)S(1)}, u32[]{:S(2)}) copy-start(bf16[8,32,768]{2,1,0:T(8,128)(2,1)S(1)} %all_gather.7) | copy-start | bytes 1179652
  50.9 31.3 %collective-permute-start.8 = (bf16[6,32,384]{2,1,0:T(8,128)(2,1)S(1)}, bf16[6,32,384]{2,1,0:T(8,128)(2,1)S(1)}, u32[]{:S(2)}, u32[]{:S(2)}) collective-permute-start(bf16[6,32,384]{2,1,0:T(8,128)(2,1)S(1)} %get-tuple-element.548), channel_id=1, source_target_pairs={{0,128},{128,256},{256,384},{384,0},{1,129},{129,257},{257,385},{3... | collective-permute-start | bytes 442376 | tf_op jit(solution)/shard_map/ppermute | solution.py:281
  56.1 17.1 %copy-start.38 = (f32[20]{0:T(128)}, f32[20]{0:T(128)S(1)}, u32[]{:S(2)}) copy-start(f32[20]{0:T(128)S(1)} %and_convert_fusion) | copy-start | bytes 244
  57.8 13.3 %collective-permute-start.6 = (bf16[20,6]{1,0:T(8,128)(2,1)S(1)}, bf16[20,6]{1,0:T(8,128)(2,1)S(1)}, u32[]{:S(2)}, u32[]{:S(2)}) collective-permute-start(bf16[20,6]{1,0:T(8,128)(2,1)S(1)} %get-tuple-element.556), channel_id=1, source_target_pairs={{0,4},{4,8},{8,12},{12,16},{16,20},{20,24},{24,28},{28,32},{32,36}... | collective-permute-start | bytes 728 | tf_op jit(solution)/shard_map/ppermute | solution.py:281
  60.0 13.0 %collective-permute-start.7 = (bf16[20,6]{1,0:T(8,128)(2,1)S(1)}, bf16[20,6]{1,0:T(8,128)(2,1)S(1)}, u32[]{:S(2)}, u32[]{:S(2)}) collective-permute-start(bf16[20,6]{1,0:T(8,128)(2,1)S(1)} %get-tuple-element.557), channel_id=1, source_target_pairs={{4,0},{8,4},{12,8},{16,12},{20,16},{24,20},{28,24},{32,28},{36,32}... | collective-permute-start | bytes 728 | tf_op jit(solution)/shard_map/ppermute | solution.py:283
  71.1 11.1 %collective-permute-start.9 = (bf16[6,32,384]{2,1,0:T(8,128)(2,1)S(1)}, bf16[6,32,384]{2,1,0:T(8,128)(2,1)S(1)}, u32[]{:S(2)}, u32[]{:S(2)}) collective-permute-start(bf16[6,32,384]{2,1,0:T(8,128)(2,1)S(1)} %get-tuple-element.549), channel_id=1, source_target_pairs={{128,0},{256,128},{384,256},{0,384},{129,1},{257,129},{385,257},{1... | collective-permute-start | bytes 442376 | tf_op jit(solution)/shard_map/ppermute | solution.py:283
  73.3 18.8 %collective-permute-start.2 = (bf16[20,6,384]{2,1,0:T(8,128)(2,1)S(1)}, bf16[20,6,384]{2,1,0:T(8,128)(2,1)S(1)}, u32[]{:S(2)}, u32[]{:S(2)}) collective-permute-start(bf16[20,6,384]{2,1,0:T(8,128)(2,1)S(1)} %get-tuple-element.542), channel_id=1, source_target_pairs={{0,4},{4,8},{8,12},{12,16},{16,20},{20,24},{24,28},{28,32},{32,36}... | collective-permute-start | bytes 276488 | tf_op jit(solution)/shard_map/ppermute | solution.py:281
  75.2 16.9 %collective-permute-start.3 = (bf16[20,6,384]{2,1,0:T(8,128)(2,1)S(1)}, bf16[20,6,384]{2,1,0:T(8,128)(2,1)S(1)}, u32[]{:S(2)}, u32[]{:S(2)}) collective-permute-start(bf16[20,6,384]{2,1,0:T(8,128)(2,1)S(1)} %get-tuple-element.543), channel_id=1, source_target_pairs={{4,0},{8,4},{12,8},{16,12},{20,16},{24,20},{28,24},{32,28},{36,32}... | collective-permute-start | bytes 276488 | tf_op jit(solution)/shard_map/ppermute | solution.py:283
  82.2 9.9 %copy-start.28 = (bf16[6,32,384]{2,1,0:T(8,128)(2,1)}, bf16[6,32,384]{2,1,0:T(8,128)(2,1)S(1)}, u32[]{:S(2)}) copy-start(bf16[6,32,384]{2,1,0:T(8,128)(2,1)S(1)} %collective-permute-done.9) | copy-start | bytes 442372
  83.0 42.7 %collective-permute-start.10 = (bf16[20,6,384]{2,1,0:T(8,128)(2,1)}, bf16[20,6,384]{2,1,0:T(8,128)(2,1)}, u32[]{:S(2)}, u32[]{:S(2)}) collective-permute-start(bf16[20,6,384]{2,1,0:T(8,128)(2,1)} %get-tuple-element.540), channel_id=1, source_target_pairs={{0,4},{4,8},{8,12},{12,16},{16,20},{20,24},{24,28},{28,32},{32,36}... | collective-permute-start | bytes 276488 | tf_op jit(solution)/shard_map/ppermute | solution.py:281
  85.0 7.7 %copy-start.8 = (pred[128,560]{0,1:T(8,128)(4,1)S(1)}, pred[128,560]{0,1:T(8,128)(4,1)}, u32[]{:S(2)}) copy-start(pred[128,560]{0,1:T(8,128)(4,1)} %constant.242.clone..sunk.4) | copy-start | bytes 215044
  85.0 40.7 %collective-permute-start.11 = (bf16[20,6,384]{2,1,0:T(8,128)(2,1)}, bf16[20,6,384]{2,1,0:T(8,128)(2,1)}, u32[]{:S(2)}, u32[]{:S(2)}) collective-permute-start(bf16[20,6,384]{2,1,0:T(8,128)(2,1)} %get-tuple-element.541), channel_id=1, source_target_pairs={{4,0},{8,4},{12,8},{16,12},{20,16},{24,20},{28,24},{32,28},{36,32}... | collective-permute-start | bytes 276488 | tf_op jit(solution)/shard_map/ppermute | solution.py:283
  114.2 11.5 %copy-start.27 = (bf16[6,32,384]{2,1,0:T(8,128)(2,1)S(1)}, bf16[6,32,384]{2,1,0:T(8,128)(2,1)}, u32[]{:S(2)}) copy-start(bf16[6,32,384]{2,1,0:T(8,128)(2,1)} %copy-done.26) | copy-start | bytes 442372
  114.2 11.5 %copy-start.29 = (bf16[6,32,384]{2,1,0:T(8,128)(2,1)S(1)}, bf16[6,32,384]{2,1,0:T(8,128)(2,1)}, u32[]{:S(2)}) copy-start(bf16[6,32,384]{2,1,0:T(8,128)(2,1)} %copy-done.28) | copy-start | bytes 442372
  115.3 23.4 %copy-start.15 = (bf16[1,8,2,16,192]{4,3,2,1,0:T(8,128)(2,1)}, bf16[1,8,2,16,192]{4,3,2,1,0:T(8,128)(2,1)S(1)}, u32[]{:S(2)}) copy-start(bf16[1,8,2,16,192]{4,3,2,1,0:T(8,128)(2,1)S(1)} %copy.92) | copy-start | bytes 294916
  119.0 9.2 %collective-permute-start.12 = (f32[6,32,6]{1,0,2:T(8,128)S(1)}, f32[6,32,6]{1,0,2:T(8,128)S(1)}, u32[]{:S(2)}, u32[]{:S(2)}) collective-permute-start(f32[6,32,6]{1,0,2:T(8,128)S(1)} %get-tuple-element.554), channel_id=1, source_target_pairs={{0,128},{128,256},{256,384},{384,0},{1,129},{129,257},{257,385},{3... | collective-permute-start | bytes 13832 | tf_op jit(solution)/shard_map/ppermute | solution.py:281
  123.8 5.1 %collective-permute-start.13 = (f32[6,32,6]{1,0,2:T(8,128)S(1)}, f32[6,32,6]{1,0,2:T(8,128)S(1)}, u32[]{:S(2)}, u32[]{:S(2)}) collective-permute-start(f32[6,32,6]{1,0,2:T(8,128)S(1)} %get-tuple-element.555), channel_id=1, source_target_pairs={{128,0},{256,128},{384,256},{0,384},{129,1},{257,129},{385,257},{1... | collective-permute-start | bytes 13832 | tf_op jit(solution)/shard_map/ppermute | solution.py:283
  127.0 11.7 %copy-start.25 = (bf16[192,768]{1,0:T(8,128)(2,1)S(1)}, bf16[192,768]{1,0:T(8,128)(2,1)}, u32[]{:S(2)}) copy-start(bf16[192,768]{1,0:T(8,128)(2,1)} %param.13) | copy-start | bytes 884740
  128.2 13.8 %copy-start.39 = (f32[20]{0:T(128)S(1)}, f32[20]{0:T(128)}, u32[]{:S(2)}) copy-start(f32[20]{0:T(128)} %copy-done.38) | copy-start | bytes 244
  129.7 10.2 %collective-permute-start.14 = (f32[20,6,6]{1,0,2:T(8,128)S(1)}, f32[20,6,6]{1,0,2:T(8,128)S(1)}, u32[]{:S(2)}, u32[]{:S(2)}) collective-permute-start(f32[20,6,6]{1,0,2:T(8,128)S(1)} %get-tuple-element.552), channel_id=1, source_target_pairs={{0,4},{4,8},{8,12},{12,16},{16,20},{20,24},{24,28},{28,32},{32,36}... | collective-permute-start | bytes 8648 | tf_op jit(solution)/shard_map/ppermute | solution.py:281
  131.7 8.8 %collective-permute-start.15 = (f32[20,6,6]{1,0,2:T(8,128)S(1)}, f32[20,6,6]{1,0,2:T(8,128)S(1)}, u32[]{:S(2)}, u32[]{:S(2)}) collective-permute-start(f32[20,6,6]{1,0,2:T(8,128)S(1)} %get-tuple-element.553), channel_id=1, source_target_pairs={{4,0},{8,4},{12,8},{16,12},{20,16},{24,20},{28,24},{32,28},{36,32}... | collective-permute-start | bytes 8648 | tf_op jit(solution)/shard_map/ppermute | solution.py:283
  139.7 111.1 %reduce-scatter.9.cloned.1.call-start = ((), (), s32[]{:S(2)}) async-start(), calls=%async_computation.3 | async-start | bytes 491520
  143.1 6.9 %copy-start.2 = (bf16[8,32,192]{2,1,0:T(8,128)(2,1)}, bf16[8,32,192]{2,1,0:T(8,128)(2,1)S(1)}, u32[]{:S(2)}) copy-start(bf16[8,32,192]{2,1,0:T(8,128)(2,1)S(1)} %get-tuple-element.861) | copy-start | bytes 294916 | tf_op jit(solution)/shard_map/while
  143.1 6.9 %copy-start.6 = (bf16[8,32,192]{2,1,0:T(8,128)(2,1)}, bf16[8,32,192]{2,1,0:T(8,128)(2,1)S(1)}, u32[]{:S(2)}) copy-start(bf16[8,32,192]{2,1,0:T(8,128)(2,1)S(1)} %get-tuple-element.863) | copy-start | bytes 294916 | tf_op jit(solution)/shard_map/while
  143.1 7.7 %copy-start.18 = (f32[20,44]{1,0:T(8,128)}, f32[20,44]{1,0:T(8,128)S(1)}, u32[]{:S(2)}) copy-start(f32[20,44]{1,0:T(8,128)S(1)} %get-tuple-element.860) | copy-start | bytes 10564 | tf_op jit(solution)/shard_map/while
  143.1 8.7 %copy-start.9 = (pred[128,560]{0,1:T(8,128)(4,1)}, pred[128,560]{0,1:T(8,128)(4,1)S(1)}, u32[]{:S(2)}) copy-start(pred[128,560]{0,1:T(8,128)(4,1)S(1)} %get-tuple-element.877) | copy-start | bytes 215044 | tf_op jit(solution)/shard_map/while
  143.1 16.1 %copy-start.20 = (f32[20,44,3]{1,0,2:T(8,128)}, f32[20,44,3]{1,0,2:T(8,128)S(1)}, u32[]{:S(2)}) copy-start(f32[20,44,3]{1,0,2:T(8,128)S(1)} %get-tuple-element.871) | copy-start | bytes 31684 | tf_op jit(solution)/shard_map/while
  150.5 5.6 %copy-start.4 = (bf16[20,44,192]{2,1,0:T(8,128)(2,1)S(1)}, bf16[20,44,192]{2,1,0:T(8,128)(2,1)}, u32[]{:S(2)}) copy-start(bf16[20,44,192]{2,1,0:T(8,128)(2,1)} %get-tuple-element.870) | copy-start | bytes 1013764 | tf_op jit(solution)/shard_map/while
  150.5 5.6 %copy-start.5 = (bf16[20,44,192]{2,1,0:T(8,128)(2,1)S(1)}, bf16[20,44,192]{2,1,0:T(8,128)(2,1)}, u32[]{:S(2)}) copy-start(bf16[20,44,192]{2,1,0:T(8,128)(2,1)} %get-tuple-element.866) | copy-start | bytes 1013764 | tf_op jit(solution)/shard_map/while
  166.8 6.9 %copy-start.2 = (bf16[8,32,192]{2,1,0:T(8,128)(2,1)}, bf16[8,32,192]{2,1,0:T(8,128)(2,1)S(1)}, u32[]{:S(2)}) copy-start(bf16[8,32,192]{2,1,0:T(8,128)(2,1)S(1)} %get-tuple-element.861) | copy-start | bytes 294916 | tf_op jit(solution)/shard_map/while
  166.8 6.9 %copy-start.6 = (bf16[8,32,192]{2,1,0:T(8,128)(2,1)}, bf16[8,32,192]{2,1,0:T(8,128)(2,1)S(1)}, u32[]{:S(2)}) copy-start(bf16[8,32,192]{2,1,0:T(8,128)(2,1)S(1)} %get-tuple-element.863) | copy-start | bytes 294916 | tf_op jit(solution)/shard_map/while
  166.8 7.7 %copy-start.18 = (f32[20,44]{1,0:T(8,128)}, f32[20,44]{1,0:T(8,128)S(1)}, u32[]{:S(2)}) copy-start(f32[20,44]{1,0:T(8,128)S(1)} %get-tuple-element.860) | copy-start | bytes 10564 | tf_op jit(solution)/shard_map/while
  166.8 8.7 %copy-start.9 = (pred[128,560]{0,1:T(8,128)(4,1)}, pred[128,560]{0,1:T(8,128)(4,1)S(1)}, u32[]{:S(2)}) copy-start(pred[128,560]{0,1:T(8,128)(4,1)S(1)} %get-tuple-element.877) | copy-start | bytes 215044 | tf_op jit(solution)/shard_map/while
  166.8 16.1 %copy-start.20 = (f32[20,44,3]{1,0,2:T(8,128)}, f32[20,44,3]{1,0,2:T(8,128)S(1)}, u32[]{:S(2)}) copy-start(f32[20,44,3]{1,0,2:T(8,128)S(1)} %get-tuple-element.871) | copy-start | bytes 31684 | tf_op jit(solution)/shard_map/while
  174.2 5.6 %copy-start.4 = (bf16[20,44,192]{2,1,0:T(8,128)(2,1)S(1)}, bf16[20,44,192]{2,1,0:T(8,128)(2,1)}, u32[]{:S(2)}) copy-start(bf16[20,44,192]{2,1,0:T(8,128)(2,1)} %get-tuple-element.870) | copy-start | bytes 1013764 | tf_op jit(solution)/shard_map/while
  174.2 5.6 %copy-start.5 = (bf16[20,44,192]{2,1,0:T(8,128)(2,1)S(1)}, bf16[20,44,192]{2,1,0:T(8,128)(2,1)}, u32[]{:S(2)}) copy-start(bf16[20,44,192]{2,1,0:T(8,128)(2,1)} %get-tuple-element.866) | copy-start | bytes 1013764 | tf_op jit(solution)/shard_map/while
  247.5 4.2 %copy-start.17 = (f32[8,32,768]{2,1,0:T(8,128)S(1)}, f32[8,32,768]{2,1,0:T(8,128)}, u32[]{:S(2)}) copy-start(f32[8,32,768]{2,1,0:T(8,128)} %get-tuple-element.544) | copy-start | bytes 2359300
  247.5 4.4 %copy-start.32 = (bf16[8,8,768]{2,1,0:T(8,128)(2,1)S(1)}, bf16[8,8,768]{2,1,0:T(8,128)(2,1)}, u32[]{:S(2)}) copy-start(bf16[8,8,768]{2,1,0:T(8,128)(2,1)} %param.15) | copy-start | bytes 294916
  247.5 4.4 %copy-start.36 = (f32[8,8]{1,0:T(8,128)S(1)}, f32[8,8]{1,0:T(8,128)}, u32[]{:S(2)}) copy-start(f32[8,8]{1,0:T(8,128)} %constant_dynamic-slice_fusion.15) | copy-start | bytes 772
  (28 other events, 59.9 us)
Sparse Core Ops, SparseCore 0:
  139.8 15.5 reduce-scatter.6
  193.4 21.2 reduce-scatter.8

commit v2 on v1

v2 whole, which is shorter than its diff:
```python
import jax
import jax.numpy as jnp
from jax import lax
from jax.experimental import pallas as pl
from jax.experimental.pallas import tpu as pltpu
from jax.sharding import PartitionSpec as P

MESH = pl.DeviceIdType.MESH
HEAD_SIZE = 64
REACH = 6
EPSILON = 1e-05
NEGATIVE = -1e30
N_HEAD = 4
N_LAT = 4
N_LON = 32
CELLS = 64
FULL = 768
TALL = 160
AROUND = 3 * TALL
N_Z = 16
N_Y = 4
N_OWN = 9


class Place:
    def __init__(self):
        self.lat = lax.axis_index("lat")
        self.lon = lax.axis_index("lon")
        self.head = lax.axis_index("head")
        self.core = lax.rem(self.lat, 2)
        self.y = (self.lon // N_Z) * 2 + self.lat // 2
        self.z = lax.rem(self.lon, N_Z)

    def at(self, core=None, y=None, z=None):
        core = self.core if core is None else core
        y = self.y if y is None else y
        z = self.z if z is None else z
        return (lax.rem(y, 2) * 2 + core, (y // 2) * N_Z + z, self.head)


    def beside(self, step_lat, step_lon):
        return (self.lat + step_lat, lax.rem(self.lon + step_lon + N_LON, N_LON), self.head)

    def peer(self, head):
        return (self.lat, self.lon, head)


def remote(src, dst, send_sem, recv_sem, device):
    return pltpu.make_async_remote_copy(
        src_ref=src,
        dst_ref=dst,
        send_sem=send_sem,
        recv_sem=recv_sem,
        device_id=device,
        device_id_type=MESH,
    )


class Summed:
    def __init__(self, place, turn, src, res, cbuf, ybuf, zbuf, sem_c, sem_y, sem_z, sem_zg, sem_yg, sem_cg):
        self.p = place
        self.src, self.res, self.cbuf, self.ybuf, self.zbuf = src, res, cbuf, ybuf, zbuf
        self.sem_c, self.sem_y, self.sem_z = sem_c, sem_y, sem_z
        self.sem_zg, self.sem_yg, self.sem_cg = sem_zg, sem_yg, sem_cg
        self.turn = turn
        turned = lax.rem(place.z + N_Z - turn, N_Z)
        self.mine = (turned * N_OWN + N_Z - 1) // N_Z
        self.owner = (self.mine * N_Z) // N_OWN == turned
        self.mine = jnp.minimum(self.mine, N_OWN - 1)

    @staticmethod
    def scratch(t):
        bf = jnp.bfloat16
        return [
            pltpu.VMEM((2, N_Y, N_OWN, t, 128), bf),
            pltpu.VMEM((2, N_Y, N_OWN, t, 128), bf),
            pltpu.VMEM((N_Y, N_OWN, t, 128), bf),
            pltpu.VMEM((N_Y, N_OWN, t, 128), bf),
            pltpu.VMEM((N_Z, t, 128), bf),
            pltpu.SemaphoreType.DMA((2,)),
            pltpu.SemaphoreType.DMA((2, N_Y)),
            pltpu.SemaphoreType.DMA((2, N_Z)),
            pltpu.SemaphoreType.DMA((2, N_Z)),
            pltpu.SemaphoreType.DMA((2, N_Y)),
            pltpu.SemaphoreType.DMA((2, N_Y)),
        ]

    def core_copy(self):
        p = self.p
        return remote(
            self.src.at[1 - p.core], self.cbuf, self.sem_c.at[0], self.sem_c.at[1], p.at(core=1 - p.core)
        )

    def y_copy(self, step, arriving=False):
        p = self.p
        y = lax.rem(p.y + step, N_Y)
        slot = y if arriving else p.y
        return remote(
            self.src.at[p.core, y], self.ybuf.at[slot], self.sem_y.at[0, y], self.sem_y.at[1, slot], p.at(y=y)
        )

    def owner_z(self, tile):
        return lax.rem((tile * N_Z) // N_OWN + self.turn, N_Z)

    def z_copy(self, tile):
        p = self.p
        return remote(
            self.src.at[p.core, p.y, tile],
            self.zbuf.at[p.z],
            self.sem_z.at[0, tile],
            self.sem_z.at[1, p.z],
            p.at(z=self.owner_z(tile)),
        )

    def z_arrival(self, z):
        p = self.p
        return remote(
            self.src.at[p.core, p.y, 0], self.zbuf.at[z], self.sem_z.at[0, 0], self.sem_z.at[1, z], p.at(z=z)
        )

    def zg_copy(self, z, tile):
        p = self.p
        here = self.res.at[p.core, p.y, tile]
        return remote(here, here, self.sem_zg.at[0, z], self.sem_zg.at[1, tile], p.at(z=z))

    def yg_copy(self, step, arriving=False):
        p = self.p
        y = lax.rem(p.y + step, N_Y)
        slot = y if arriving else p.y
        here = self.res.at[p.core, slot]
        return remote(here, here, self.sem_yg.at[0, y], self.sem_yg.at[1, slot], p.at(y=y))

    def cg_copy(self, y, arriving=False):
        p = self.p
        here = self.res.at[1 - p.core if arriving else p.core, y]
        return remote(here, here, self.sem_cg.at[0, y], self.sem_cg.at[1, y], p.at(core=1 - p.core))

    def send_core(self):
        self.core_copy().start()

    def core_to_y(self):
        p = self.p
        self.core_copy().wait_recv()
        for step in (2, 1, 3, 0):
            y = lax.rem(p.y + step, N_Y)
            both = self.src[p.core, y].astype(jnp.float32) + self.cbuf[y].astype(jnp.float32)
            self.src[p.core, y] = both.astype(jnp.bfloat16)
            if step:
                self.y_copy(step).start()

    def y_to_z(self):
        p = self.p
        for step in (1, 3, 2):
            self.y_copy(step, True).wait_recv()
        total = self.src[p.core, p.y].astype(jnp.float32)
        for step in (1, 2, 3):
            total = total + self.ybuf[lax.rem(p.y + step, N_Y)].astype(jnp.float32)
        self.src[p.core, p.y] = total.astype(jnp.bfloat16)

        @pl.loop(0, N_OWN)
        def _(tile):
            @pl.when(self.owner_z(tile) != p.z)
            def _():
                self.z_copy(tile).start()

    def z_to_all(self):
        p = self.p

        @pl.when(self.owner)
        def _():
            @pl.loop(1, N_Z)
            def _(step):
                self.z_arrival(lax.rem(p.z + step, N_Z)).wait_recv()

            def add(step, total):
                return total + self.zbuf[lax.rem(p.z + step, N_Z)].astype(jnp.float32)

            own = self.src[p.core, p.y, self.mine].astype(jnp.float32)
            total = lax.fori_loop(1, N_Z, add, own)
            self.res[p.core, p.y, self.mine] = total.astype(jnp.bfloat16)

            @pl.loop(1, N_Z)
            def _(step):
                self.zg_copy(lax.rem(p.z + step, N_Z), self.mine).start()

    def all_to_y(self):
        p = self.p

        @pl.loop(0, N_OWN)
        def _(tile):
            @pl.when(self.owner_z(tile) != p.z)
            def _():
                self.zg_copy(0, tile).wait_recv()

        for step in (2, 1, 3):
            self.yg_copy(step).start()
        self.cg_copy(p.y).start()

    def y_to_core(self):
        p = self.p
        for step in (1, 3, 2):
            self.yg_copy(step, True).wait_recv()
            self.cg_copy(lax.rem(p.y + step, N_Y)).start()

    def finish(self):
        p = self.p
        for y in range(N_Y):
            self.cg_copy(y, True).wait_recv()
        self.core_copy().wait_send()
        for step in (1, 2, 3):
            self.y_copy(step).wait_send()
            self.yg_copy(step).wait_send()
        for y in range(N_Y):
            self.cg_copy(y).wait_send()

        @pl.loop(0, N_OWN)
        def _(tile):
            @pl.when(self.owner_z(tile) != p.z)
            def _():
                self.z_copy(tile).wait_send()

        @pl.when(self.owner)
        def _():
            @pl.loop(1, N_Z)
            def _(step):
                self.zg_copy(lax.rem(p.z + step, N_Z), self.mine).wait_send()


def dot(a, b):
    return lax.dot_general(a, b, (((1,), (0,)), ((), ())), preferred_element_type=jnp.float32)


def dot_rows(a, b):
    return lax.dot_general(a, b, (((1,), (1,)), ((), ())), preferred_element_type=jnp.float32)


def dot_cells(a, b):
    return lax.dot_general(a, b, (((0,), (0,)), ((), ())), preferred_element_type=jnp.float32)


def half(values):
    return values.astype(jnp.bfloat16)


def wide(values):
    return values.astype(jnp.float32)


class Halo:
    def __init__(self, place, ref, sems, by_block):
        self.p, self.ref, self.sems, self.by_block = place, ref, sems, by_block

    def message(self, index, block, src_rows, dst_block, dst_rows, step_lat, step_lon):
        src = self.ref.at[block, pl.ds(*src_rows)]
        dst = self.ref.at[dst_block, pl.ds(*dst_rows)]
        device = self.p.beside(step_lat, step_lon)
        return remote(src, dst, self.sems.at[0, index], self.sems.at[1, index], device)

    def north(self, block):
        at = block + 1 if self.by_block else pl.ds(1, 4)
        return self.message(block, at, (48, 48), at, (112, 48), -1, 0)

    def south(self, block):
        at = block + 1 if self.by_block else pl.ds(1, 4)
        return self.message(4 + block, at, (64, 48), at, (0, 48), 1, 0)

    def side(self, row, east):
        src_rows, dst_rows = {0: ((48, 64), (48, 64)), -1: ((48, 48), (112, 48)), 1: ((64, 48), (0, 48))}[row]
        index = 8 + 2 * (row % 3) + east
        return self.message(index, 4 if east else 1, src_rows, 0 if east else 5, dst_rows, row, 1 if east else -1)

    def when(self, row, then):
        if row == -1:
            pl.when(self.p.lat > 0)(then)
        elif row == 1:
            pl.when(self.p.lat < N_LAT - 1)(then)
        else:
            then()

    def send_rows(self, block):
        self.when(-1, lambda: self.north(block).start())
        self.when(1, lambda: self.south(block).start())

    def send_side(self, east):
        for row in (0, -1, 1):
            self.when(row, lambda row=row: self.side(row, east).start())

    def send_all(self):
        self.send_rows(0)
        self.send_side(0)
        self.send_side(1)

    def blocks(self):
        return range(4) if self.by_block else range(1)

    def wait_all(self):
        for block in self.blocks():
            self.when(1, lambda block=block: self.north(block).wait_recv())
            self.when(-1, lambda block=block: self.south(block).wait_recv())
        for east in (0, 1):
            for row in (0, -1, 1):
                self.when(-row, lambda row=row, east=east: self.side(row, east).wait_recv())

    def wait_sent(self):
        for block in self.blocks():
            self.when(-1, lambda block=block: self.north(block).wait_send())
            self.when(1, lambda block=block: self.south(block).wait_send())
        for east in (0, 1):
            for row in (0, -1, 1):
                self.when(row, lambda row=row, east=east: self.side(row, east).wait_send())


class Spread:
    def __init__(self, place, src, dst, sems):
        self.p, self.src, self.dst, self.sems = place, src, dst, sems

    def copy(self, head):
        src = self.src.at[head] if len(self.src.shape) == 3 else self.src
        return remote(
            src, self.dst.at[self.p.head], self.sems.at[0, head], self.sems.at[1, self.p.head], self.p.peer(head)
        )

    def arrival(self, head):
        src = self.src.at[head] if len(self.src.shape) == 3 else self.src
        return remote(src, self.dst.at[head], self.sems.at[0, head], self.sems.at[1, head], self.p.peer(head))

    def other(self, step):
        return lax.rem(self.p.head + step, N_HEAD)

    def wait_sent(self):
        for step in (1, 2, 3):
            self.copy(self.other(step)).wait_send()


def geometry(shape):
    row = lax.broadcasted_iota(jnp.int32, shape, 0)
    lane = lax.broadcasted_iota(jnp.int32, shape, 1)
    block = jnp.where(lane >= TALL, 1, 0) + jnp.where(lane >= 2 * TALL, 1, 0)
    rest = lane - TALL * block
    lat = (rest >> 3) - REACH
    step_lat = lat - (row >> 3)
    step_lon = (block - 1) * 8 + (rest & 7) - (row & 7)
    return lat, step_lat, step_lon


def put(src, t, top, values):
    for row in range(0, values.shape[0], t):
        y, third = (top + row) // (3 * t), (top + row) // t % 3
        for column in range(6):
            src[column // 3, y, third * 3 + column % 3] = half(
                values[row : row + t, column * 128 : column * 128 + 128]
            )


def take(res, t, top, out_ref, out_top, rows):
    for row in range(0, rows, t):
        y, third = (top + row) // (3 * t), (top + row) // t % 3
        for column in range(6):
            out_ref[out_top + row : out_top + row + t, column * 128 : column * 128 + 128] = res[
                column // 3, y, third * 3 + column % 3
            ]


T = 32
N_SUM = 11


def block_kernel(
    x_ref, gy_ref, wqkv_ref, wo_ref, valid_ref, mixed_ref, gx_ref, gqkv_ref, gwo_ref,
    ng, gg, norm32, spread, wp, wop, ext, flags, stats, mask_q, mask_k, gp, pvs, pvr, gns, gnr,
    sem_n, sem_g, sem_pv, sem_gn, sem_ext, sem_flags, sem_stats, *sums,
):
    p = Place()
    barrier = pltpu.get_barrier_semaphore()

    def greet(device):
        pl.semaphore_signal(barrier, inc=1, device_id=device, device_id_type=MESH)

    for step in range(1, N_HEAD):
        greet(p.peer(lax.rem(p.head + step, N_HEAD)))
    for step_lon in (-1, 0, 1):
        if step_lon:
            greet(p.beside(0, step_lon))

        @pl.when(p.lat > 0)
        def _():
            greet(p.beside(-1, step_lon))

        @pl.when(p.lat < N_LAT - 1)
        def _():
            greet(p.beside(1, step_lon))

    for step in range(1, N_Y):
        greet(p.at(y=lax.rem(p.y + step, N_Y)))

    @pl.loop(1, N_Z)
    def _(step):
        greet(p.at(z=lax.rem(p.z + step, N_Z)))

    early = Summed(p, 0, *sums[:N_SUM])
    late = Summed(p, 8, *sums[N_SUM:])
    normed_gather = Spread(p, ng.at[p.head], ng, sem_n)
    grad_gather = Spread(p, gg.at[p.head], gg, sem_g)
    halo = Halo(p, ext, sem_ext, True)
    flag_halo = Halo(p, flags, sem_flags, False)
    stat_halo = Halo(p, stats, sem_stats, False)

    gg[p.head] = gy_ref[...]
    values = wide(x_ref[...])
    center = values - jnp.mean(values, axis=-1, keepdims=True)
    inv = lax.rsqrt(jnp.mean(center * center, axis=-1, keepdims=True) + EPSILON)
    norm32[...] = center * inv
    spread[...] = jnp.broadcast_to(inv, spread.shape)
    ng[p.head] = half(center * inv)
    for top, at_edge in ((0, p.lat == 0), (112, p.lat == N_LAT - 1)):

        @pl.when(at_edge)
        def _():
            for ref in (ext, flags, stats):
                ref[:, top : top + 48, :] = jnp.zeros((6, 48, ref.shape[2]), jnp.bfloat16)

    row = lax.broadcasted_iota(jnp.int32, (CELLS, 8), 0)
    column = lax.broadcasted_iota(jnp.int32, (CELLS, 8), 1)
    by_lat = dot(half(jnp.where((row >> 3) == column, 1.0, 0.0)), half(wide(valid_ref[...])))
    row = lax.broadcasted_iota(jnp.int32, (CELLS, N_LON), 0)
    column = lax.broadcasted_iota(jnp.int32, (CELLS, N_LON), 1)
    for block in range(4):
        own_flag = half(jnp.where(column == 8 * block + (row & 7), by_lat, 0.0))
        flags[block + 1, 48:112] = half(dot(own_flag, jnp.ones((N_LON, 128), jnp.bfloat16)))

    greeted = 3 + 2 + 1 + (N_Y - 1) + (N_Z - 1) - 1
    edge = jnp.where(p.lat > 0, 3, 0) + jnp.where(p.lat < N_LAT - 1, 3, 0)
    pl.semaphore_wait(barrier, greeted + edge)

    for step in (1, 3, 2):
        normed_gather.copy(normed_gather.other(step)).start()
        grad_gather.copy(grad_gather.other(step)).start()
    flag_halo.send_all()

    nothing = jnp.zeros((64, FULL), jnp.bfloat16)
    for part in range(3):
        wp[128 * part : 128 * part + 128] = wqkv_ref[part, 0:128]
    wp[384:448] = wqkv_ref[0, 128:192]
    wp[448:512] = nothing
    wp[512:576] = wqkv_ref[1, 128:192]
    wp[576:640] = wqkv_ref[2, 128:192]
    wop[0:128] = wo_ref[0:128]
    wop[128:192] = nothing
    wop[192:256] = wo_ref[128:192]

    lat, step_lat, step_lon = geometry((CELLS, AROUND))
    inside = (jnp.abs(step_lat) <= REACH) & (jnp.abs(step_lon) <= REACH)
    middle = (step_lat == 0) & (step_lon == 0)
    there = lat + p.lat * 8
    inside_rows = inside & (there >= 0) & (there < 8 * N_LAT)
    for block in range(4):
        own_flag = wide(flags[block + 1, 48:112])[:, 0:1]
        mask_k[block] = jnp.where(inside_rows & ((own_flag > 0) | middle), 0.0, NEGATIVE)

    low = lax.broadcasted_iota(jnp.int32, (CELLS, 128), 1) < HEAD_SIZE
    zero = jnp.zeros((CELLS, 128), jnp.bfloat16)
    lane = lax.broadcasted_iota(jnp.int32, (CELLS, 128), 1)

    def first(values):
        return jnp.where(low, values, zero)

    def second(values):
        return jnp.where(low, zero, values)

    @pl.loop(0, N_HEAD)
    def _(step):
        order = jnp.where(step == 2, 3, jnp.where(step == 3, 2, step))
        block = lax.rem(p.head + order, N_HEAD)

        @pl.when(step > 0)
        def _():
            normed_gather.arrival(block).wait_recv()
            grad_gather.arrival(block).wait_recv()

        projected = dot_rows(ng[block], wp[...])
        d_attended = dot_rows(gg[block], wop[...])
        scale = HEAD_SIZE ** (-0.5)
        ext[block + 1, 48:112, 0:128] = half(half(projected[:, 0:128]) * scale)
        ext[block + 1, 48:112, 128:384] = half(projected[:, 128:384])
        ext[block + 1, 48:112, 384:512] = half(d_attended[:, 0:128])
        ext[block + 1, 48:112, 512:640] = jnp.where(
            low, half(projected[:, 384:512] * scale), half(d_attended[:, 128:256])
        )
        ext[block + 1, 48:112, 640:768] = half(projected[:, 512:640])
        halo.send_rows(block)

        @pl.when(block == 0)
        def _():
            halo.send_side(0)

        @pl.when(block == 3)
        def _():
            halo.send_side(1)

    flag_halo.wait_all()
    ones = half(jnp.where(lane == 0, 1.0, 0.0))
    for block in range(4):
        flag = dot_rows(ones, flags[block : block + 3].reshape(AROUND, 128))
        mask_q[block] = jnp.where(inside & ((flag > 0) | middle), 0.0, NEGATIVE)
    halo.wait_all()

    def stacked(a, b, c):
        return jnp.concatenate(
            [jnp.concatenate(part, axis=1) for part in (a, b, c)],
            axis=0,
        )

    def thrice(mask):
        return jnp.concatenate([mask, mask, mask], axis=0)

    def around(block, *groups):
        parts = [
            (stats if g == 6 else ext)[pl.ds(block, 3), :, (0 if g == 6 else g * 128) : (0 if g == 6 else g * 128) + 128]
            for g in groups
        ]
        return jnp.concatenate([part.reshape(AROUND, 128) for part in parts], axis=1)

    def own(block, group):
        return ext[block + 1, 48:112, group * 128 : group * 128 + 128]

    @pl.loop(0, 4)
    def _(block):
        keys, values = around(block, 1, 5), around(block, 2, 5)
        q01, d01, qd2 = own(block, 0), own(block, 3), own(block, 4)
        queries = stacked((first(q01), zero), (second(q01), zero), (zero, first(qd2)))
        douts = stacked((first(d01), zero), (second(d01), zero), (zero, second(qd2)))
        score = dot_rows(queries, keys) + thrice(mask_q[block])
        best = jnp.max(score, axis=1, keepdims=True)
        chance = jnp.exp(score - best)
        total = jnp.sum(chance, axis=1, keepdims=True)
        level = best + jnp.log(total)
        chance = chance * (1.0 / total)
        inner = dot_rows(douts, values)
        carried = jnp.sum(chance * inner, axis=1, keepdims=True)
        soft_grad = half(chance * (inner - carried))
        attended = dot(half(chance), values)
        grad_query = dot(soft_grad, keys) * HEAD_SIZE ** (-0.5)
        gp[block, :, 640:768] = half(jnp.where(low, attended[0:64, 0:128], attended[64:128, 0:128]))
        gp[block, :, 0:128] = half(jnp.where(low, grad_query[0:64, 0:128], grad_query[64:128, 0:128]))
        gp[block, :, 384:512] = half(jnp.where(low, grad_query[128:192, 128:256], attended[128:192, 128:256]))
        tile = jnp.zeros((CELLS, 128), jnp.float32)
        for kind, column in enumerate((level, carried)):
            for head in range(3):
                rest = column[64 * head : 64 * head + 64]
                for digit in range(3):
                    piece = wide(half(rest))
                    rest = rest - piece
                    tile = jnp.where(lane == 9 * kind + 3 * head + digit, piece, tile)
        stats[block + 1, 48:112] = half(tile)

    stat_halo.send_all()

    def cells(ref, *groups):
        return jnp.concatenate([ref[:, :, g * 128 : g * 128 + 128].reshape(4 * CELLS, 128) for g in groups], axis=1)

    grads = gg[...].reshape(4 * CELLS, FULL)
    normed = ng[...].reshape(4 * CELLS, FULL)
    mixed_in = cells(gp, 5, 3)
    weights = dot_cells(mixed_in, grads)
    put(early.src, T, 0, weights[0:128])
    put(early.src, T, 128, weights[192:256])
    weights = dot_cells(cells(gp, 0, 3), normed)
    put(early.src, T, 192, weights[0:192])
    early.send_core()

    out_spread = Spread(p, pvs, pvr, sem_pv)
    pvs[...] = half(dot(mixed_in, wop[...])).reshape(4, CELLS, FULL)
    for step in (2, 1, 3):
        out_spread.copy(out_spread.other(step)).start()
    early.core_to_y()

    stat_halo.wait_all()

    def minus_one(start):
        return half(jnp.where((lane >= start) & (lane < start + 3), -1.0, 0.0))

    def keys_side(block):
        queries, douts = around(block, 0, 4, 6), around(block, 3, 4, 6)
        k01, v01, kv2 = own(block, 1), own(block, 2), own(block, 5)
        keys = stacked(
            (first(k01), zero, minus_one(0)), (second(k01), zero, minus_one(3)), (zero, first(kv2), minus_one(6))
        )
        values = stacked(
            (first(v01), zero, minus_one(9)), (second(v01), zero, minus_one(12)), (zero, second(kv2), minus_one(15))
        )
        chance = jnp.exp(dot_rows(keys, queries) + thrice(mask_k[block]))
        soft_grad = half(chance * dot_rows(values, douts))
        grad_key = dot(soft_grad, queries[:, 0:256])
        grad_value = dot(half(chance), douts[:, 0:256])
        gp[block, :, 128:256] = half(jnp.where(low, grad_key[0:64, 0:128], grad_key[64:128, 0:128]))
        gp[block, :, 256:384] = half(jnp.where(low, grad_value[0:64, 0:128], grad_value[64:128, 0:128]))
        gp[block, :, 512:640] = half(jnp.where(low, grad_key[128:192, 128:256], grad_value[128:192, 128:256]))

    pl.loop(0, 2)(keys_side)
    early.y_to_z()
    pl.loop(2, 4)(keys_side)

    weights = dot_cells(cells(gp, 1, 4), normed)
    put(late.src, T, 0, weights[0:192])
    weights = jnp.concatenate([dot_cells(cells(gp, 2), normed), weights[192:256]], axis=0)
    put(late.src, T, 192, weights)
    late.send_core()

    norm_spread = Spread(p, gns, gnr, sem_gn)
    gns[...] = half(dot(cells(gp, 0, 1, 2, 3, 4), wp[...])).reshape(4, CELLS, FULL)
    for step in (2, 1, 3):
        norm_spread.copy(norm_spread.other(step)).start()

    early.z_to_all()
    late.core_to_y()

    total = wide(pvs[p.head])
    for step in (1, 2, 3):
        other = out_spread.other(step)
        out_spread.arrival(other).wait_recv()
        total = total + wide(pvr[other])
    mixed_ref[...] = half(wide(x_ref[...]) + total)

    early.all_to_y()
    late.y_to_z()

    total = wide(gns[p.head])
    for step in (1, 2, 3):
        other = norm_spread.other(step)
        norm_spread.arrival(other).wait_recv()
        total = total + wide(gnr[other])
    own_norm = norm32[...]
    mean = jnp.mean(total, axis=-1, keepdims=True)
    along = jnp.mean(total * own_norm, axis=-1, keepdims=True)
    d_input = spread[:, 0:1] * (total - mean - own_norm * along)
    gx_ref[...] = half(wide(gy_ref[...]) + d_input)

    late.z_to_all()
    early.y_to_core()
    late.all_to_y()
    early.finish()
    take(early.res, T, 0, gwo_ref, 0, 192)
    take(early.res, T, 192, gqkv_ref, 0, 192)
    late.y_to_core()
    for spread_copy in (normed_gather, grad_gather, out_spread, norm_spread):
        spread_copy.wait_sent()
    for one in (halo, flag_halo, stat_halo):
        one.wait_sent()
    late.finish()
    take(late.res, T, 0, gqkv_ref, 192, 384)


def on_device(activations, qkv_weight, out_weight, valid, grad_y):
    bf, f32 = jnp.bfloat16, jnp.float32
    vmem = pl.BlockSpec(memory_space=pltpu.VMEM)
    gathered = pltpu.VMEM((N_HEAD, CELLS, FULL), bf)
    pair = pltpu.SemaphoreType.DMA((2, N_HEAD))
    around = pltpu.SemaphoreType.DMA((2, 14))
    mixed, grad_x, grad_qkv, grad_out = pl.pallas_call(
        block_kernel,
        out_shape=[
            jax.ShapeDtypeStruct((CELLS, FULL), bf),
            jax.ShapeDtypeStruct((CELLS, FULL), bf),
            jax.ShapeDtypeStruct((3 * 192, FULL), bf),
            jax.ShapeDtypeStruct((192, FULL), bf),
        ],
        in_specs=[vmem] * 5,
        out_specs=[vmem] * 4,
        scratch_shapes=[
            gathered,
            gathered,
            pltpu.VMEM((CELLS, FULL), f32),
            pltpu.VMEM((CELLS, 128), f32),
            pltpu.VMEM((640, FULL), bf),
            pltpu.VMEM((256, FULL), bf),
            pltpu.VMEM((6, TALL, FULL), bf),
            pltpu.VMEM((6, TALL, 128), bf),
            pltpu.VMEM((6, TALL, 128), bf),
            pltpu.VMEM((4, CELLS, AROUND), f32),
            pltpu.VMEM((4, CELLS, AROUND), f32),
            gathered,
            gathered,
            gathered,
            gathered,
            gathered,
            pair,
            pair,
            pair,
            pair,
            around,
            around,
            around,
            *Summed.scratch(T),
            *Summed.scratch(T),
        ],
        compiler_params=pltpu.CompilerParams(
            collective_id=0, has_side_effects=True, vmem_limit_bytes=48 * 2**20
        ),
    )(
        activations.reshape(CELLS, FULL),
        grad_y.reshape(CELLS, FULL),
        qkv_weight,
        out_weight,
        valid,
    )
    return (
        mixed.reshape(activations.shape),
        grad_x.reshape(activations.shape),
        grad_qkv.reshape(qkv_weight.shape),
        grad_out,
    )


def solution(mesh):
    return jax.shard_map(
        on_device,
        mesh=mesh,
        in_specs=(
            P("lat", ("lon", "head"), None),
            P(None, "head", None),
            P("head", None),
            P("lat", "lon"),
            P("lat", ("lon", "head"), None),
        ),
        out_specs=(
            P("lat", ("lon", "head"), None),
            P("lat", ("lon", "head"), None),
            P(None, "head", None),
            P("head", None),
        ),
        check_vma=False,
    )
```

time: 261 us -> 93.2 us (0.36)
  starting transfers between devices: 71.7 us -> 0 us
  local copies, waits for them, and re-layouts: 50.9 us -> 7.5 us
  Pallas kernels: 53 us -> 83.6 us
  blocking collectives: 20.8 us -> 0 us
  matrix products: 19.9 us -> 0 us
  other arithmetic: 16.7 us -> 0 us
  between operations: 14.9 us -> 0.65 us
  loops' own time: 10.3 us -> 0 us
    ppermute x16 -> x0, starting transfers between devices: 71.4 us -> none  [the longest x8 45.2 us: extended(): lax.ppermute(head, axis, [((i + 1) % count, i) for i in range(count)])]
    pallas_call x1, Pallas kernels: 53 us -> 83.6 us  [on_device(): pl.pallas_call(block_kernel, out_shape=[jax.ShapeDtypeStruct((CELLS, FULL...]
    all_gather x2 -> x0, blocking collectives: 20.8 us -> none  [the longest x1 11.2 us: on_device(): whole = lax.all_gather(activations, 'head', axis=1, tiled=True)]
    dot_general x20 -> x0, matrix products: 19.9 us -> none  [the longest x2 4.75 us: backward_tile(): jnp.einsum('hqk,khc->qhc', soft_grad, key_block, preferred_element_type=j...]
    reshape x39 -> x0, local copies, waits for them, and re-layouts: 18.7 us -> none  [the longest x28 14.2 us: by_heads(): return piece.reshape(piece.shape[0], heads, HEAD_SIZE)]
    dynamic_slice x20 -> x0, local copies, waits for them, and re-layouts: 12.8 us -> none  [the longest x16 9.09 us: cut_block(): piece = lax.dynamic_slice(field, starts, (rows, cols) + field.shape[2:])]
    another operation x2 -> x0, loops' own time: 10.3 us -> none  [the longest x1 6.26 us: on_device(): grad_tiles = lax.map(backward_tile, tile_ids)]
    slice x16 -> x0, local copies, waits for them, and re-layouts: 5.58 us -> none  [the longest x1 1.14 us: on_device(): dout_margin = margin_pair[:, :, width:]]
  transfers between devices with their start and end apart: 18 -> 0, of which waited for: 2 -> 0; matrix products, arithmetic and copies ran while one was open for 31% -> 0% of each run, Pallas kernels for 20% -> 0%
where the time goes in v2:
time: 93.2 us; the launch traced here: 91.7 us
  Pallas kernels  83.6 us (90%)
  local copies, waits for them, and re-layouts  7.5 us (8%)
    pallas_call x1, Pallas kernels, on_device(): pl.pallas_call(block_kernel, out_shape=[jax.ShapeDtypeStruct((CELLS, FULL...  83.6 us
    unnamed x14, local copies, waits for them, and re-layouts  7.5 us

profile of v2, /device:TPU:1, one launch (start us, length us, event | category | flops | bytes accessed | tf_op | source)
XLA Modules:
  0.0 91.7 jit_solution(1043555940018272370)
XLA Ops:
  0.6 0.0 copy-start
  0.6 1.2 %copy-done = bf16[3,192,768]{2,1,0:T(8,128)(2,1)S(1)} copy-done((bf16[3,192,768]{2,1,0:T(8,128)(2,1)S(1)}, bf16[3,192,768]{2,1,0:T(8,128)(2,1)}, u32[]{:S(2)}) %copy-start) | copy-done | bytes 884760
  1.8 0.0 copy-start.1
  1.8 1.0 %copy-done.1 = bf16[192,768]{1,0:T(8,128)(2,1)S(1)} copy-done((bf16[192,768]{1,0:T(8,128)(2,1)S(1)}, bf16[192,768]{1,0:T(8,128)(2,1)}, u32[]{:S(2)}) %copy-start.1) | copy-done | bytes 294936
  2.8 0.0 copy-start.2
  2.8 0.9 copy-done.2
  3.7 0.0 copy-start.3
  3.7 0.9 copy-done.3
  4.5 0.0 copy-start.4
  4.6 0.7 copy-done.4
  5.2 83.6 %shard_map.84 = (bf16[64,768]{1,0:T(8,128)(2,1)S(1)}, bf16[64,768]{1,0:T(8,128)(2,1)S(1)}, bf16[576,768]{1,0:T(8,128)(2,1)S(1)}, bf16[192,768]{1,0:T(8,128)(2,1)S(1)}) custom-call(bf16[64,768]{1,0:T(8,128)(2,1)S(1)} %bitcast.8, bf16[64,768]{1,0:T(8,128)(2,1)S(1)} %bitcast.9, bf16[3,192,768]{2,1,0:T(8,128)(2,1)S(1)} %copy-done, ...), custom_call_target="tpu_custom_call" | custom-call | tf_op jit(solution)/shard_map/pallas_call | solution.py:659
  88.8 0.6 copy.13
  89.4 0.6 copy.14
  90.1 0.9 copy.15
  91.0 0.7 copy.16
Async XLA Ops:
  0.6 1.2 %copy-start = (bf16[3,192,768]{2,1,0:T(8,128)(2,1)S(1)}, bf16[3,192,768]{2,1,0:T(8,128)(2,1)}, u32[]{:S(2)}) copy-start(bf16[3,192,768]{2,1,0:T(8,128)(2,1)} %wqkv_ref.1) | copy-start | bytes 2654212
  1.8 1.0 %copy-start.1 = (bf16[192,768]{1,0:T(8,128)(2,1)S(1)}, bf16[192,768]{1,0:T(8,128)(2,1)}, u32[]{:S(2)}) copy-start(bf16[192,768]{1,0:T(8,128)(2,1)} %wo_ref.1) | copy-start | bytes 884740
  2.8 0.9 copy-start.2
  3.7 0.9 copy-start.3
  4.5 0.7 copy-start.4

commit v3 on v2

--- a/solution.py
+++ b/solution.py
@@ -366,16 +366,50 @@
 
 
 def block_kernel(
-    x_ref, gy_ref, wqkv_ref, wo_ref, valid_ref, mixed_ref, gx_ref, gqkv_ref, gwo_ref,
-    ng, gg, norm32, spread, wp, wop, ext, flags, stats, mask_q, mask_k, gp, pvs, pvr, gns, gnr,
-    sem_n, sem_g, sem_pv, sem_gn, sem_ext, sem_flags, sem_stats, *sums,
+    x_ref, gy_ref, wqkv_ref, wo_ref, valid_ref, mixed_out, gx_out, gqkv_out, gwo_out,
+    mixed_ref, gx_ref, gqkv_ref, gwo_ref, sem_out, xv, valid_v, ng, gg, norm32, spread, wp, wop, ext, dext, stats, mask_q, mask_k, gp, pvs, pvr, gns, gnr,
+    sem_in, sem_n, sem_g, sem_pv, sem_gn, sem_ext, sem_dext, sem_stats, *sums,
 ):
     p = Place()
     barrier = pltpu.get_barrier_semaphore()
+    loads = [
+        pltpu.make_async_copy(src, dst, sem_in.at[index])
+        for index, (src, dst) in enumerate(
+            (
+                (x_ref, xv),
+                (valid_ref, valid_v),
+                (gy_ref, gg.at[p.head]),
+                (wqkv_ref.at[0, pl.ds(0, 128)], wp.at[pl.ds(0, 128)]),
+                (wqkv_ref.at[1, pl.ds(0, 128)], wp.at[pl.ds(128, 128)]),
+                (wqkv_ref.at[2, pl.ds(0, 128)], wp.at[pl.ds(256, 128)]),
+                (wqkv_ref.at[0, pl.ds(128, 64)], wp.at[pl.ds(384, 64)]),
+                (wqkv_ref.at[1, pl.ds(128, 64)], wp.at[pl.ds(512, 64)]),
+                (wqkv_ref.at[2, pl.ds(128, 64)], wp.at[pl.ds(576, 64)]),
+                (wo_ref.at[pl.ds(0, 128)], wop.at[pl.ds(0, 128)]),
+                (wo_ref.at[pl.ds(128, 64)], wop.at[pl.ds(192, 64)]),
+            )
+        )
+    ]
+
+    query_rows, rest = pl.ds(0, 192), pl.ds(192, 384)
+    mixed_store, gx_store, gwo_store, query_store, rest_store = [
+        pltpu.make_async_copy(src, dst, sem_out.at[index])
+        for index, (src, dst) in enumerate(
+            (
+                (mixed_ref, mixed_out),
+                (gx_ref, gx_out),
+                (gwo_ref, gwo_out),
+                (gqkv_ref.at[query_rows], gqkv_out.at[query_rows]),
+                (gqkv_ref.at[rest], gqkv_out.at[rest]),
+            )
+        )
+    ]
 
     def greet(device):
         pl.semaphore_signal(barrier, inc=1, device_id=device, device_id_type=MESH)
 
+    for load in loads:
+        load.start()
     for step in range(1, N_HEAD):
         greet(p.peer(lax.rem(p.head + step, N_HEAD)))
     for step_lon in (-1, 0, 1):
@@ -402,11 +436,11 @@
     normed_gather = Spread(p, ng.at[p.head], ng, sem_n)
     grad_gather = Spread(p, gg.at[p.head], gg, sem_g)
     halo = Halo(p, ext, sem_ext, True)
-    flag_halo = Halo(p, flags, sem_flags, False)
+    dout_halo = Halo(p, dext, sem_dext, True)
     stat_halo = Halo(p, stats, sem_stats, False)
 
-    gg[p.head] = gy_ref[...]
-    values = wide(x_ref[...])
+    loads[0].wait()
+    values = wide(xv[...])
     center = values - jnp.mean(values, axis=-1, keepdims=True)
     inv = lax.rsqrt(jnp.mean(center * center, axis=-1, keepdims=True) + EPSILON)
     norm32[...] = center * inv
@@ -416,50 +450,43 @@
 
         @pl.when(at_edge)
         def _():
-            for ref in (ext, flags, stats):
+            for ref in (ext, dext, stats):
                 ref[:, top : top + 48, :] = jnp.zeros((6, 48, ref.shape[2]), jnp.bfloat16)
 
-    row = lax.broadcasted_iota(jnp.int32, (CELLS, 8), 0)
-    column = lax.broadcasted_iota(jnp.int32, (CELLS, 8), 1)
-    by_lat = dot(half(jnp.where((row >> 3) == column, 1.0, 0.0)), half(wide(valid_ref[...])))
-    row = lax.broadcasted_iota(jnp.int32, (CELLS, N_LON), 0)
-    column = lax.broadcasted_iota(jnp.int32, (CELLS, N_LON), 1)
-    for block in range(4):
-        own_flag = half(jnp.where(column == 8 * block + (row & 7), by_lat, 0.0))
-        flags[block + 1, 48:112] = half(dot(own_flag, jnp.ones((N_LON, 128), jnp.bfloat16)))
-
-    greeted = 3 + 2 + 1 + (N_Y - 1) + (N_Z - 1) - 1
-    edge = jnp.where(p.lat > 0, 3, 0) + jnp.where(p.lat < N_LAT - 1, 3, 0)
-    pl.semaphore_wait(barrier, greeted + edge)
-
-    for step in (1, 3, 2):
-        normed_gather.copy(normed_gather.other(step)).start()
-        grad_gather.copy(grad_gather.other(step)).start()
-    flag_halo.send_all()
-
-    nothing = jnp.zeros((64, FULL), jnp.bfloat16)
-    for part in range(3):
-        wp[128 * part : 128 * part + 128] = wqkv_ref[part, 0:128]
-    wp[384:448] = wqkv_ref[0, 128:192]
-    wp[448:512] = nothing
-    wp[512:576] = wqkv_ref[1, 128:192]
-    wp[576:640] = wqkv_ref[2, 128:192]
-    wop[0:128] = wo_ref[0:128]
-    wop[128:192] = nothing
-    wop[192:256] = wo_ref[128:192]
-
+    loads[1].wait()
+    low = lax.broadcasted_iota(jnp.int32, (CELLS, 128), 1) < HEAD_SIZE
+    zero = jnp.zeros((CELLS, 128), jnp.bfloat16)
+    lane = lax.broadcasted_iota(jnp.int32, (CELLS, 128), 1)
     lat, step_lat, step_lon = geometry((CELLS, AROUND))
     inside = (jnp.abs(step_lat) <= REACH) & (jnp.abs(step_lon) <= REACH)
     middle = (step_lat == 0) & (step_lon == 0)
     there = lat + p.lat * 8
     inside_rows = inside & (there >= 0) & (there < 8 * N_LAT)
+    row = lax.broadcasted_iota(jnp.int32, (CELLS, 8), 0)
+    column = lax.broadcasted_iota(jnp.int32, (CELLS, 8), 1)
+    by_lat = dot(half(jnp.where((row >> 3) == column, 1.0, 0.0)), half(wide(valid_v[...])))
+    row = lax.broadcasted_iota(jnp.int32, (CELLS, N_LON), 0)
+    column = lax.broadcasted_iota(jnp.int32, (CELLS, N_LON), 1)
     for block in range(4):
-        own_flag = wide(flags[block + 1, 48:112])[:, 0:1]
-        mask_k[block] = jnp.where(inside_rows & ((own_flag > 0) | middle), 0.0, NEGATIVE)
-
-    low = lax.broadcasted_iota(jnp.int32, (CELLS, 128), 1) < HEAD_SIZE
-    zero = jnp.zeros((CELLS, 128), jnp.bfloat16)
-    lane = lax.broadcasted_iota(jnp.int32, (CELLS, 128), 1)
+        own_flag = half(jnp.where(column == 8 * block + (row & 7), by_lat, 0.0))
+        flag = dot(own_flag, jnp.ones((N_LON, 128), jnp.bfloat16))
+        ext[block + 1, 48:112, 512:640] = half(flag)
+        mask_k[block] = jnp.where(inside_rows & ((flag[:, 0:1] > 0) | middle), 0.0, NEGATIVE)
+
+    greeted = 3 + 2 + 1 + (N_Y - 1) + (N_Z - 1) - 1
+    edge = jnp.where(p.lat > 0, 3, 0) + jnp.where(p.lat < N_LAT - 1, 3, 0)
+    pl.semaphore_wait(barrier, greeted + edge)
+
+    for step in (1, 3, 2):
+        normed_gather.copy(normed_gather.other(step)).start()
+    loads[2].wait()
+    for step in (1, 3, 2):
+        grad_gather.copy(grad_gather.other(step)).start()
+
+    wp[448:512] = jnp.zeros((64, FULL), jnp.bfloat16)
+    wop[128:192] = jnp.zeros((64, FULL), jnp.bfloat16)
+    for load in loads[3:]:
+        load.wait()
 
     def first(values):
         return jnp.where(low, values, zero)
@@ -467,42 +494,52 @@
     def second(values):
         return jnp.where(low, zero, values)
 
-    @pl.loop(0, N_HEAD)
-    def _(step):
+    def arrived(step, gather, margins, project):
         order = jnp.where(step == 2, 3, jnp.where(step == 3, 2, step))
         block = lax.rem(p.head + order, N_HEAD)
 
         @pl.when(step > 0)
         def _():
-            normed_gather.arrival(block).wait_recv()
-            grad_gather.arrival(block).wait_recv()
-
+            gather.arrival(block).wait_recv()
+
+        project(block)
+        margins.send_rows(block)
+
+        @pl.when(block == 0)
+        def _():
+            margins.send_side(0)
+
+        @pl.when(block == 3)
+        def _():
+            margins.send_side(1)
+
+    def project_normed(block):
         projected = dot_rows(ng[block], wp[...])
-        d_attended = dot_rows(gg[block], wop[...])
         scale = HEAD_SIZE ** (-0.5)
         ext[block + 1, 48:112, 0:128] = half(half(projected[:, 0:128]) * scale)
         ext[block + 1, 48:112, 128:384] = half(projected[:, 128:384])
-        ext[block + 1, 48:112, 384:512] = half(d_attended[:, 0:128])
+        ext[block + 1, 48:112, 384:512] = half(projected[:, 512:640])
         ext[block + 1, 48:112, 512:640] = jnp.where(
-            low, half(projected[:, 384:512] * scale), half(d_attended[:, 128:256])
-        )
-        ext[block + 1, 48:112, 640:768] = half(projected[:, 512:640])
-        halo.send_rows(block)
-
-        @pl.when(block == 0)
-        def _():
-            halo.send_side(0)
-
-        @pl.when(block == 3)
-        def _():
-            halo.send_side(1)
-
-    flag_halo.wait_all()
-    ones = half(jnp.where(lane == 0, 1.0, 0.0))
+            low, half(projected[:, 384:512] * scale), ext[block + 1, 48:112, 512:640]
+        )
+
+    def project_grad(block):
+        dext[block + 1, 48:112] = half(dot_rows(gg[block], wop[...]))
+
+    @pl.loop(0, N_HEAD)
+    def _(step):
+        arrived(step, normed_gather, halo, project_normed)
+
+    @pl.loop(0, N_HEAD)
+    def _(step):
+        arrived(step, grad_gather, dout_halo, project_grad)
+
+    halo.wait_all()
+    pick = half(jnp.where(lane == HEAD_SIZE, 1.0, 0.0))
     for block in range(4):
-        flag = dot_rows(ones, flags[block : block + 3].reshape(AROUND, 128))
+        flag = dot_rows(pick, ext[block : block + 3, :, 512:640].reshape(AROUND, 128))
         mask_q[block] = jnp.where(inside & ((flag > 0) | middle), 0.0, NEGATIVE)
-    halo.wait_all()
+    dout_halo.wait_all()
 
     def stacked(a, b, c):
         return jnp.concatenate(
@@ -515,20 +552,23 @@
 
     def around(block, *groups):
         parts = [
-            (stats if g == 6 else ext)[pl.ds(block, 3), :, (0 if g == 6 else g * 128) : (0 if g == 6 else g * 128) + 128]
-            for g in groups
+            ref[pl.ds(block, 3), :, group * 128 : group * 128 + 128].reshape(AROUND, 128) for ref, group in groups
         ]
-        return jnp.concatenate([part.reshape(AROUND, 128) for part in parts], axis=1)
-
-    def own(block, group):
-        return ext[block + 1, 48:112, group * 128 : group * 128 + 128]
+        return jnp.concatenate(parts, axis=1)
+
+    def own(block, ref, group):
+        return ref[block + 1, 48:112, group * 128 : group * 128 + 128]
+
+    Q01, K01, V01, KV2, Q2 = ((ext, group) for group in range(5))
+    D01, D2 = (dext, 0), (dext, 1)
+    STAT = (stats, 0)
 
     @pl.loop(0, 4)
     def _(block):
-        keys, values = around(block, 1, 5), around(block, 2, 5)
-        q01, d01, qd2 = own(block, 0), own(block, 3), own(block, 4)
-        queries = stacked((first(q01), zero), (second(q01), zero), (zero, first(qd2)))
-        douts = stacked((first(d01), zero), (second(d01), zero), (zero, second(qd2)))
+        keys, values = around(block, K01, KV2), around(block, V01, KV2)
+        q01, d01 = own(block, *Q01), own(block, *D01)
+        queries = stacked((first(q01), zero), (second(q01), zero), (zero, first(own(block, *Q2))))
+        douts = stacked((first(d01), zero), (second(d01), zero), (zero, own(block, *D2)))
         score = dot_rows(queries, keys) + thrice(mask_q[block])
         best = jnp.max(score, axis=1, keepdims=True)
         chance = jnp.exp(score - best)
@@ -573,15 +613,14 @@
     for step in (2, 1, 3):
         out_spread.copy(out_spread.other(step)).start()
     early.core_to_y()
-
     stat_halo.wait_all()
 
     def minus_one(start):
         return half(jnp.where((lane >= start) & (lane < start + 3), -1.0, 0.0))
 
     def keys_side(block):
-        queries, douts = around(block, 0, 4, 6), around(block, 3, 4, 6)
-        k01, v01, kv2 = own(block, 1), own(block, 2), own(block, 5)
+        queries, douts = around(block, Q01, Q2, STAT), around(block, D01, D2, STAT)
+        k01, v01, kv2 = own(block, *K01), own(block, *V01), own(block, *KV2)
         keys = stacked(
             (first(k01), zero, minus_one(0)), (second(k01), zero, minus_one(3)), (zero, first(kv2), minus_one(6))
         )
@@ -596,33 +635,33 @@
         gp[block, :, 256:384] = half(jnp.where(low, grad_value[0:64, 0:128], grad_value[64:128, 0:128]))
         gp[block, :, 512:640] = half(jnp.where(low, grad_key[128:192, 128:256], grad_value[128:192, 128:256]))
 
-    pl.loop(0, 2)(keys_side)
-    early.y_to_z()
-    pl.loop(2, 4)(keys_side)
+    pl.loop(0, 4)(keys_side)
 
     weights = dot_cells(cells(gp, 1, 4), normed)
     put(late.src, T, 0, weights[0:192])
     weights = jnp.concatenate([dot_cells(cells(gp, 2), normed), weights[192:256]], axis=0)
     put(late.src, T, 192, weights)
     late.send_core()
+    early.y_to_z()
 
     norm_spread = Spread(p, gns, gnr, sem_gn)
     gns[...] = half(dot(cells(gp, 0, 1, 2, 3, 4), wp[...])).reshape(4, CELLS, FULL)
     for step in (2, 1, 3):
         norm_spread.copy(norm_spread.other(step)).start()
 
+    late.core_to_y()
     early.z_to_all()
-    late.core_to_y()
 
     total = wide(pvs[p.head])
     for step in (1, 2, 3):
         other = out_spread.other(step)
         out_spread.arrival(other).wait_recv()
         total = total + wide(pvr[other])
-    mixed_ref[...] = half(wide(x_ref[...]) + total)
-
+    mixed_ref[...] = half(wide(xv[...]) + total)
+    mixed_store.start()
+
+    late.y_to_z()
     early.all_to_y()
-    late.y_to_z()
 
     total = wide(gns[p.head])
     for step in (1, 2, 3):
@@ -633,30 +672,48 @@
     mean = jnp.mean(total, axis=-1, keepdims=True)
     along = jnp.mean(total * own_norm, axis=-1, keepdims=True)
     d_input = spread[:, 0:1] * (total - mean - own_norm * along)
-    gx_ref[...] = half(wide(gy_ref[...]) + d_input)
+    gx_ref[...] = half(wide(gg[p.head]) + d_input)
+    gx_store.start()
 
     late.z_to_all()
     early.y_to_core()
+    for spread_copy in (normed_gather, grad_gather, out_spread, norm_spread):
+        spread_copy.wait_sent()
+    for one in (halo, dout_halo, stat_halo):
+        one.wait_sent()
     late.all_to_y()
     early.finish()
     take(early.res, T, 0, gwo_ref, 0, 192)
     take(early.res, T, 192, gqkv_ref, 0, 192)
+    gwo_store.start()
+    query_store.start()
     late.y_to_core()
-    for spread_copy in (normed_gather, grad_gather, out_spread, norm_spread):
-        spread_copy.wait_sent()
-    for one in (halo, flag_halo, stat_halo):
-        one.wait_sent()
     late.finish()
     take(late.res, T, 0, gqkv_ref, 192, 384)
+    rest_store.start()
+    for store in (mixed_store, gx_store, gwo_store, query_store, rest_store):
+        store.wait()
+
+
+def store_kernel(*refs):
+    given, out, held, sems = refs[:4], refs[4:8], refs[8:12], refs[12]
+    loads = [pltpu.make_async_copy(given[i], held[i], sems.at[0, i]) for i in range(4)]
+    stores = [pltpu.make_async_copy(held[i], out[i], sems.at[1, i]) for i in range(4)]
+    for load in loads:
+        load.start()
+    for load, store in zip(loads, stores):
+        load.wait()
+        store.start()
+    for store in stores:
+        store.wait()
 
 
 def on_device(activations, qkv_weight, out_weight, valid, grad_y):
     bf, f32 = jnp.bfloat16, jnp.float32
-    vmem = pl.BlockSpec(memory_space=pltpu.VMEM)
     gathered = pltpu.VMEM((N_HEAD, CELLS, FULL), bf)
     pair = pltpu.SemaphoreType.DMA((2, N_HEAD))
     around = pltpu.SemaphoreType.DMA((2, 14))
-    mixed, grad_x, grad_qkv, grad_out = pl.pallas_call(
+    results = pl.pallas_call(
         block_kernel,
         out_shape=[
             jax.ShapeDtypeStruct((CELLS, FULL), bf),
@@ -664,17 +721,24 @@
             jax.ShapeDtypeStruct((3 * 192, FULL), bf),
             jax.ShapeDtypeStruct((192, FULL), bf),
         ],
-        in_specs=[vmem] * 5,
-        out_specs=[vmem] * 4,
+        in_specs=[pl.BlockSpec(memory_space=pltpu.HBM)] * 5,
+        out_specs=[pl.BlockSpec(memory_space=pltpu.HBM)] * 4,
         scratch_shapes=[
+            pltpu.VMEM((CELLS, FULL), bf),
+            pltpu.VMEM((CELLS, FULL), bf),
+            pltpu.VMEM((3 * 192, FULL), bf),
+            pltpu.VMEM((192, FULL), bf),
+            pltpu.SemaphoreType.DMA((5,)),
+            pltpu.VMEM((CELLS, FULL), bf),
+            pltpu.VMEM((8, N_LON), jnp.int32),
             gathered,
             gathered,
             pltpu.VMEM((CELLS, FULL), f32),
             pltpu.VMEM((CELLS, 128), f32),
             pltpu.VMEM((640, FULL), bf),
             pltpu.VMEM((256, FULL), bf),
-            pltpu.VMEM((6, TALL, FULL), bf),
-            pltpu.VMEM((6, TALL, 128), bf),
+            pltpu.VMEM((6, TALL, 640), bf),
+            pltpu.VMEM((6, TALL, 256), bf),
             pltpu.VMEM((6, TALL, 128), bf),
             pltpu.VMEM((4, CELLS, AROUND), f32),
             pltpu.VMEM((4, CELLS, AROUND), f32),
@@ -683,6 +747,7 @@
             gathered,
             gathered,
             gathered,
+            pltpu.SemaphoreType.DMA((11,)),
             pair,
             pair,
             pair,
@@ -694,7 +759,7 @@
             *Summed.scratch(T),
         ],
         compiler_params=pltpu.CompilerParams(
-            collective_id=0, has_side_effects=True, vmem_limit_bytes=48 * 2**20
+            collective_id=0, has_side_effects=True, vmem_limit_bytes=63 * 2**20
         ),
     )(
         activations.reshape(CELLS, FULL),
@@ -703,6 +768,16 @@
         out_weight,
         valid,
     )
+    mixed, grad_x, grad_qkv, grad_out = pl.pallas_call(
+        store_kernel,
+        out_shape=[jax.ShapeDtypeStruct(result.shape, bf) for result in results],
+        in_specs=[pl.BlockSpec(memory_space=pl.ANY)] * 4,
+        out_specs=[pl.BlockSpec(memory_space=pltpu.HBM)] * 4,
+        scratch_shapes=[
+            *(pltpu.VMEM(result.shape, bf) for result in results),
+            pltpu.SemaphoreType.DMA((2, 4)),
+        ],
+    )(*results)
     return (
         mixed.reshape(activations.shape),
         grad_x.reshape(activations.shape),

time: 93.2 us -> 82.5 us (0.89); the launches traced: 91.7 us -> 82.3 us
  local copies, waits for them, and re-layouts: 7.5 us -> 0 us
  Pallas kernels: 83.6 us -> 81.7 us
    unnamed x14 -> x0, local copies, waits for them, and re-layouts: 7.5 us -> none
    pallas_call x1, Pallas kernels: 83.6 us -> 79.4 us  [on_device(): pl.pallas_call(block_kernel, out_shape=[jax.ShapeDtypeStruct((CELLS, FULL...]
    pallas_call x0 -> x1, Pallas kernels: none -> 2.35 us  [on_device(): pl.pallas_call(store_kernel, out_shape=[jax.ShapeDtypeStruct(result.shape...]
where the time goes in v3:
time: 82.5 us; the launch traced here: 82.3 us
  Pallas kernels  81.7 us (99%)
    pallas_call x1, Pallas kernels, on_device(): pl.pallas_call(block_kernel, out_shape=[jax.ShapeDtypeStruct((CELLS, FULL...  79.4 us
    pallas_call x1, Pallas kernels, on_device(): pl.pallas_call(store_kernel, out_shape=[jax.ShapeDtypeStruct(result.shape...  2.35 us

profile of v3, /device:TPU:1, one launch (start us, length us, event | category | flops | bytes accessed | tf_op | source)
XLA Modules:
  0.0 82.3 jit_solution(12856017385851388144)
XLA Ops:
  0.6 79.4 %shard_map.84 = (bf16[64,768]{1,0:T(8,128)(2,1)}, bf16[64,768]{1,0:T(8,128)(2,1)}, bf16[576,768]{1,0:T(8,128)(2,1)}, bf16[192,768]{1,0:T(8,128)(2,1)}) custom-call(bf16[64,768]{1,0:T(8,128)(2,1)} %bitcast.5, bf16[64,768]{1,0:T(8,128)(2,1)} %bitcast.6, bf16[3,192,768]{2,1,0:T(8,128)(2,1)} %wqkv_ref.1, bf16[192,768]{1,0:T(8,128)(2,1)} %wo_ref.1, s32[8,32]{1,0:T(8,128)} %valid_ref.1), custom_call_target="tpu_custom_call" | custom-call | tf_op jit(solution)/shard_map/pallas_call | solution.py:716
  80.0 2.4 %shard_map.85 = (bf16[64,768]{1,0:T(8,128)(2,1)}, bf16[64,768]{1,0:T(8,128)(2,1)}, bf16[576,768]{1,0:T(8,128)(2,1)}, bf16[192,768]{1,0:T(8,128)(2,1)}) custom-call(bf16[64,768]{1,0:T(8,128)(2,1)} %get-tuple-element.12.refs_0_, bf16[64,768]{1,0:T(8,128)(2,1)} %get-tuple-element.13.refs_1_, bf16[576,768]{1,0:T(8,128)(2,1)} %get-tuple-element.14.refs_2_, ...), custom_call_target="tpu_custom_call" | custom-call | tf_op jit(solution)/shard_map/pallas_call | solution.py:771

commit v4 on v3

--- a/solution.py
+++ b/solution.py
@@ -19,7 +19,9 @@
 AROUND = 3 * TALL
 N_Z = 16
 N_Y = 4
-N_OWN = 9
+NEAR = 4
+CHUNK = 5
+TILES = NEAR * CHUNK
 
 
 class Place:
@@ -57,33 +59,46 @@
 
 
 class Summed:
-    def __init__(self, place, turn, src, res, cbuf, ybuf, zbuf, sem_c, sem_y, sem_z, sem_zg, sem_yg, sem_cg):
+    def __init__(self, place, src, res, cbuf, ybuf, nbuf, fbuf, sem_c, sem_y, sem_n, sem_f, sem_ng, sem_yg, sem_cg):
         self.p = place
-        self.src, self.res, self.cbuf, self.ybuf, self.zbuf = src, res, cbuf, ybuf, zbuf
-        self.sem_c, self.sem_y, self.sem_z = sem_c, sem_y, sem_z
-        self.sem_zg, self.sem_yg, self.sem_cg = sem_zg, sem_yg, sem_cg
-        self.turn = turn
-        turned = lax.rem(place.z + N_Z - turn, N_Z)
-        self.mine = (turned * N_OWN + N_Z - 1) // N_Z
-        self.owner = (self.mine * N_Z) // N_OWN == turned
-        self.mine = jnp.minimum(self.mine, N_OWN - 1)
+        self.src, self.res, self.cbuf, self.ybuf, self.nbuf, self.fbuf = src, res, cbuf, ybuf, nbuf, fbuf
+        self.sem_c, self.sem_y, self.sem_n, self.sem_f = sem_c, sem_y, sem_n, sem_f
+        self.sem_ng, self.sem_yg, self.sem_cg = sem_ng, sem_yg, sem_cg
+        self.two = jnp.where(place.core == 0, 2, N_Z - 2)
 
     @staticmethod
-    def scratch(t):
+    def scratch():
         bf = jnp.bfloat16
+        sems = pltpu.SemaphoreType.DMA
         return [
-            pltpu.VMEM((2, N_Y, N_OWN, t, 128), bf),
-            pltpu.VMEM((2, N_Y, N_OWN, t, 128), bf),
-            pltpu.VMEM((N_Y, N_OWN, t, 128), bf),
-            pltpu.VMEM((N_Y, N_OWN, t, 128), bf),
-            pltpu.VMEM((N_Z, t, 128), bf),
-            pltpu.SemaphoreType.DMA((2,)),
-            pltpu.SemaphoreType.DMA((2, N_Y)),
-            pltpu.SemaphoreType.DMA((2, N_Z)),
-            pltpu.SemaphoreType.DMA((2, N_Z)),
-            pltpu.SemaphoreType.DMA((2, N_Y)),
-            pltpu.SemaphoreType.DMA((2, N_Y)),
+            pltpu.VMEM((2, N_Y, TILES, 16, 128), bf),
+            pltpu.VMEM((2, N_Y, TILES, 16, 128), bf),
+            pltpu.VMEM((N_Y, TILES, 16, 128), bf),
+            pltpu.VMEM((N_Y, TILES, 16, 128), bf),
+            pltpu.VMEM((NEAR, CHUNK, 16, 128), bf),
+            pltpu.VMEM((NEAR, CHUNK, 16, 128), bf),
+            sems((2,)),
+            sems((2, N_Y, NEAR)),
+            sems((2, NEAR)),
+            sems((2, NEAR)),
+            sems((2, NEAR)),
+            sems((2, N_Y, NEAR)),
+            sems((2, N_Y)),
         ]
+
+    def clear(self):
+        for ref in (self.src,):
+            ref[:, :, 18:TILES] = jnp.zeros((2, N_Y, TILES - 18, 16, 128), jnp.bfloat16)
+
+    def chunk(self, away):
+        return lax.rem(self.p.z + away, NEAR)
+
+    def tiles(self, away):
+        return pl.ds(CHUNK * self.chunk(away), CHUNK)
+
+    def along(self, away):
+        step = {1: 1, 2: self.two, 3: N_Z - 1}[away]
+        return lax.rem(self.p.z + step, N_Z), lax.rem(self.p.z + N_Z - step, N_Z)
 
     def core_copy(self):
         p = self.p
@@ -91,44 +106,53 @@
             self.src.at[1 - p.core], self.cbuf, self.sem_c.at[0], self.sem_c.at[1], p.at(core=1 - p.core)
         )
 
-    def y_copy(self, step, arriving=False):
+    def y_copy(self, step, away, arriving=False):
         p = self.p
         y = lax.rem(p.y + step, N_Y)
         slot = y if arriving else p.y
         return remote(
-            self.src.at[p.core, y], self.ybuf.at[slot], self.sem_y.at[0, y], self.sem_y.at[1, slot], p.at(y=y)
-        )
-
-    def owner_z(self, tile):
-        return lax.rem((tile * N_Z) // N_OWN + self.turn, N_Z)
-
-    def z_copy(self, tile):
-        p = self.p
+            self.src.at[p.core, y, self.tiles(away)],
+            self.ybuf.at[slot, self.tiles(away)],
+            self.sem_y.at[0, y, away],
+            self.sem_y.at[1, slot, away],
+            p.at(y=y),
+        )
+
+    def near_copy(self, away):
+        p = self.p
+        there, _ = self.along(away)
         return remote(
-            self.src.at[p.core, p.y, tile],
-            self.zbuf.at[p.z],
-            self.sem_z.at[0, tile],
-            self.sem_z.at[1, p.z],
-            p.at(z=self.owner_z(tile)),
-        )
-
-    def z_arrival(self, z):
-        p = self.p
+            self.src.at[p.core, p.y, self.tiles(away)],
+            self.nbuf.at[away],
+            self.sem_n.at[0, away],
+            self.sem_n.at[1, away],
+            p.at(z=there),
+        )
+
+    def far_copy(self, step, arriving=False):
+        p = self.p
+        z = lax.rem(p.z + 4 * step, N_Z)
+        slot = (z if arriving else p.z) // 4
         return remote(
-            self.src.at[p.core, p.y, 0], self.zbuf.at[z], self.sem_z.at[0, 0], self.sem_z.at[1, z], p.at(z=z)
-        )
-
-    def zg_copy(self, z, tile):
-        p = self.p
-        here = self.res.at[p.core, p.y, tile]
-        return remote(here, here, self.sem_zg.at[0, z], self.sem_zg.at[1, tile], p.at(z=z))
-
-    def yg_copy(self, step, arriving=False):
+            self.src.at[p.core, p.y, self.tiles(0)],
+            self.fbuf.at[slot],
+            self.sem_f.at[0, step],
+            self.sem_f.at[1, slot],
+            p.at(z=z),
+        )
+
+    def back_copy(self, away, arriving=False):
+        p = self.p
+        _, there = self.along(away)
+        here = self.res.at[p.core, p.y, self.tiles(away if arriving else 0)]
+        return remote(here, here, self.sem_ng.at[0, away], self.sem_ng.at[1, away], p.at(z=there))
+
+    def yg_copy(self, step, away, arriving=False):
         p = self.p
         y = lax.rem(p.y + step, N_Y)
         slot = y if arriving else p.y
-        here = self.res.at[p.core, slot]
-        return remote(here, here, self.sem_yg.at[0, y], self.sem_yg.at[1, slot], p.at(y=y))
+        here = self.res.at[p.core, slot, self.tiles(away)]
+        return remote(here, here, self.sem_yg.at[0, y, away], self.sem_yg.at[1, slot, away], p.at(y=y))
 
     def cg_copy(self, y, arriving=False):
         p = self.p
@@ -145,85 +169,77 @@
             y = lax.rem(p.y + step, N_Y)
             both = self.src[p.core, y].astype(jnp.float32) + self.cbuf[y].astype(jnp.float32)
             self.src[p.core, y] = both.astype(jnp.bfloat16)
-            if step:
-                self.y_copy(step).start()
-
-    def y_to_z(self):
+        for away in (2, 1, 3, 0):
+            for step in (2, 1, 3):
+                self.y_copy(step, away).start()
+
+    def y_to_near(self):
+        p = self.p
+        for away in (2, 1, 3, 0):
+            for step in (1, 3, 2):
+                self.y_copy(step, away, True).wait_recv()
+            tiles = self.tiles(away)
+            total = self.src[p.core, p.y, tiles].astype(jnp.float32)
+            for step in (1, 2, 3):
+                total = total + self.ybuf[lax.rem(p.y + step, N_Y), tiles].astype(jnp.float32)
+            self.src[p.core, p.y, tiles] = total.astype(jnp.bfloat16)
+            if away:
+                self.near_copy(away).start()
+
+    def near_to_far(self):
+        p = self.p
+        total = self.src[p.core, p.y, self.tiles(0)].astype(jnp.float32)
+        for away in (1, 3, 2):
+            self.near_copy(away).wait_recv()
+            total = total + self.nbuf[away].astype(jnp.float32)
+        total = total.astype(jnp.bfloat16)
+        self.src[p.core, p.y, self.tiles(0)] = total
+        for step in (2, 1, 3):
+            self.far_copy(step).start()
+        self.fbuf[p.z // 4] = total
+
+    def far_to_all(self):
         p = self.p
         for step in (1, 3, 2):
-            self.y_copy(step, True).wait_recv()
-        total = self.src[p.core, p.y].astype(jnp.float32)
-        for step in (1, 2, 3):
-            total = total + self.ybuf[lax.rem(p.y + step, N_Y)].astype(jnp.float32)
-        self.src[p.core, p.y] = total.astype(jnp.bfloat16)
-
-        @pl.loop(0, N_OWN)
-        def _(tile):
-            @pl.when(self.owner_z(tile) != p.z)
-            def _():
-                self.z_copy(tile).start()
-
-    def z_to_all(self):
-        p = self.p
-
-        @pl.when(self.owner)
-        def _():
-            @pl.loop(1, N_Z)
-            def _(step):
-                self.z_arrival(lax.rem(p.z + step, N_Z)).wait_recv()
-
-            def add(step, total):
-                return total + self.zbuf[lax.rem(p.z + step, N_Z)].astype(jnp.float32)
-
-            own = self.src[p.core, p.y, self.mine].astype(jnp.float32)
-            total = lax.fori_loop(1, N_Z, add, own)
-            self.res[p.core, p.y, self.mine] = total.astype(jnp.bfloat16)
-
-            @pl.loop(1, N_Z)
-            def _(step):
-                self.zg_copy(lax.rem(p.z + step, N_Z), self.mine).start()
+            self.far_copy(step, True).wait_recv()
+        total = self.fbuf[0].astype(jnp.float32)
+        for group in range(1, NEAR):
+            total = total + self.fbuf[group].astype(jnp.float32)
+        self.res[p.core, p.y, self.tiles(0)] = total.astype(jnp.bfloat16)
+        for away in (2, 1, 3):
+            self.back_copy(away).start()
+        for step in (2, 1, 3):
+            self.yg_copy(step, 0).start()
 
     def all_to_y(self):
-        p = self.p
-
-        @pl.loop(0, N_OWN)
-        def _(tile):
-            @pl.when(self.owner_z(tile) != p.z)
-            def _():
-                self.zg_copy(0, tile).wait_recv()
-
-        for step in (2, 1, 3):
-            self.yg_copy(step).start()
-        self.cg_copy(p.y).start()
+        for away in (1, 3, 2):
+            self.back_copy(away, True).wait_recv()
+            for step in (2, 1, 3):
+                self.yg_copy(step, away).start()
+        self.cg_copy(self.p.y).start()
 
     def y_to_core(self):
         p = self.p
         for step in (1, 3, 2):
-            self.yg_copy(step, True).wait_recv()
+            for away in range(NEAR):
+                self.yg_copy(step, away, True).wait_recv()
             self.cg_copy(lax.rem(p.y + step, N_Y)).start()
 
     def finish(self):
-        p = self.p
         for y in range(N_Y):
             self.cg_copy(y, True).wait_recv()
+
+    def wait_sent(self):
         self.core_copy().wait_send()
         for step in (1, 2, 3):
-            self.y_copy(step).wait_send()
-            self.yg_copy(step).wait_send()
+            for away in range(NEAR):
+                self.y_copy(step, away).wait_send()
+                self.yg_copy(step, away).wait_send()
+            self.near_copy(step).wait_send()
+            self.far_copy(step).wait_send()
+            self.back_copy(step).wait_send()
         for y in range(N_Y):
             self.cg_copy(y).wait_send()
-
-        @pl.loop(0, N_OWN)
-        def _(tile):
-            @pl.when(self.owner_z(tile) != p.z)
-            def _():
-                self.z_copy(tile).wait_send()
-
-        @pl.when(self.owner)
-        def _():
-            @pl.loop(1, N_Z)
-            def _(step):
-                self.zg_copy(lax.rem(p.z + step, N_Z), self.mine).wait_send()
 
 
 def dot(a, b):
@@ -343,26 +359,25 @@
     return lat, step_lat, step_lon
 
 
-def put(src, t, top, values):
-    for row in range(0, values.shape[0], t):
-        y, third = (top + row) // (3 * t), (top + row) // t % 3
+def place_of(row, column):
+    return column // 3, row // 96, row % 96 // 16 * 3 + column % 3
+
+
+def put(src, top, values):
+    for row in range(0, values.shape[0], 16):
         for column in range(6):
-            src[column // 3, y, third * 3 + column % 3] = half(
-                values[row : row + t, column * 128 : column * 128 + 128]
-            )
-
-
-def take(res, t, top, out_ref, out_top, rows):
-    for row in range(0, rows, t):
-        y, third = (top + row) // (3 * t), (top + row) // t % 3
+            src[place_of(top + row, column)] = half(values[row : row + 16, column * 128 : column * 128 + 128])
+
+
+def take(res, top, out_ref, out_top, rows):
+    for row in range(0, rows, 16):
         for column in range(6):
-            out_ref[out_top + row : out_top + row + t, column * 128 : column * 128 + 128] = res[
-                column // 3, y, third * 3 + column % 3
+            out_ref[out_top + row : out_top + row + 16, column * 128 : column * 128 + 128] = res[
+                place_of(top + row, column)
             ]
 
 
-T = 32
-N_SUM = 11
+N_SUM = 13
 
 
 def block_kernel(
@@ -427,12 +442,11 @@
     for step in range(1, N_Y):
         greet(p.at(y=lax.rem(p.y + step, N_Y)))
 
-    @pl.loop(1, N_Z)
-    def _(step):
+    for step in (1, 2, 4, 8, 12, 14, 15):
         greet(p.at(z=lax.rem(p.z + step, N_Z)))
 
-    early = Summed(p, 0, *sums[:N_SUM])
-    late = Summed(p, 8, *sums[N_SUM:])
+    early = Summed(p, *sums[:N_SUM])
+    late = Summed(p, *sums[N_SUM:])
     normed_gather = Spread(p, ng.at[p.head], ng, sem_n)
     grad_gather = Spread(p, gg.at[p.head], gg, sem_g)
     halo = Halo(p, ext, sem_ext, True)
@@ -452,6 +466,16 @@
         def _():
             for ref in (ext, dext, stats):
                 ref[:, top : top + 48, :] = jnp.zeros((6, 48, ref.shape[2]), jnp.bfloat16)
+
+    greeted = 3 + 2 + (N_Y - 1) + 7
+    edge = jnp.where(p.lat > 0, 3, 0) + jnp.where(p.lat < N_LAT - 1, 3, 0)
+    pl.semaphore_wait(barrier, greeted + edge)
+
+    for step in (1, 3, 2):
+        normed_gather.copy(normed_gather.other(step)).start()
+    loads[2].wait()
+    for step in (1, 3, 2):
+        grad_gather.copy(grad_gather.other(step)).start()
 
     loads[1].wait()
     low = lax.broadcasted_iota(jnp.int32, (CELLS, 128), 1) < HEAD_SIZE
@@ -473,16 +497,8 @@
         ext[block + 1, 48:112, 512:640] = half(flag)
         mask_k[block] = jnp.where(inside_rows & ((flag[:, 0:1] > 0) | middle), 0.0, NEGATIVE)
 
-    greeted = 3 + 2 + 1 + (N_Y - 1) + (N_Z - 1) - 1
-    edge = jnp.where(p.lat > 0, 3, 0) + jnp.where(p.lat < N_LAT - 1, 3, 0)
-    pl.semaphore_wait(barrier, greeted + edge)
-
-    for step in (1, 3, 2):
-        normed_gather.copy(normed_gather.other(step)).start()
-    loads[2].wait()
-    for step in (1, 3, 2):
-        grad_gather.copy(grad_gather.other(step)).start()
-
+    early.clear()
+    late.clear()
     wp[448:512] = jnp.zeros((64, FULL), jnp.bfloat16)
     wop[128:192] = jnp.zeros((64, FULL), jnp.bfloat16)
     for load in loads[3:]:
@@ -563,8 +579,7 @@
     D01, D2 = (dext, 0), (dext, 1)
     STAT = (stats, 0)
 
-    @pl.loop(0, 4)
-    def _(block):
+    def queries_side(block):
         keys, values = around(block, K01, KV2), around(block, V01, KV2)
         q01, d01 = own(block, *Q01), own(block, *D01)
         queries = stacked((first(q01), zero), (second(q01), zero), (zero, first(own(block, *Q2))))
@@ -593,6 +608,8 @@
                     tile = jnp.where(lane == 9 * kind + 3 * head + digit, piece, tile)
         stats[block + 1, 48:112] = half(tile)
 
+    for block in range(4):
+        queries_side(block)
     stat_halo.send_all()
 
     def cells(ref, *groups):
@@ -602,10 +619,10 @@
     normed = ng[...].reshape(4 * CELLS, FULL)
     mixed_in = cells(gp, 5, 3)
     weights = dot_cells(mixed_in, grads)
-    put(early.src, T, 0, weights[0:128])
-    put(early.src, T, 128, weights[192:256])
+    put(early.src, 0, weights[0:128])
+    put(early.src, 128, weights[192:256])
     weights = dot_cells(cells(gp, 0, 3), normed)
-    put(early.src, T, 192, weights[0:192])
+    put(early.src, 192, weights[0:192])
     early.send_core()
 
     out_spread = Spread(p, pvs, pvr, sem_pv)
@@ -635,14 +652,15 @@
         gp[block, :, 256:384] = half(jnp.where(low, grad_value[0:64, 0:128], grad_value[64:128, 0:128]))
         gp[block, :, 512:640] = half(jnp.where(low, grad_key[128:192, 128:256], grad_value[128:192, 128:256]))
 
-    pl.loop(0, 4)(keys_side)
+    for block in range(4):
+        keys_side(block)
 
     weights = dot_cells(cells(gp, 1, 4), normed)
-    put(late.src, T, 0, weights[0:192])
+    put(late.src, 0, weights[0:192])
     weights = jnp.concatenate([dot_cells(cells(gp, 2), normed), weights[192:256]], axis=0)
-    put(late.src, T, 192, weights)
+    put(late.src, 192, weights)
     late.send_core()
-    early.y_to_z()
+    early.y_to_near()
 
     norm_spread = Spread(p, gns, gnr, sem_gn)
     gns[...] = half(dot(cells(gp, 0, 1, 2, 3, 4), wp[...])).reshape(4, CELLS, FULL)
@@ -650,7 +668,7 @@
         norm_spread.copy(norm_spread.other(step)).start()
 
     late.core_to_y()
-    early.z_to_all()
+    early.near_to_far()
 
     total = wide(pvs[p.head])
     for step in (1, 2, 3):
@@ -660,8 +678,9 @@
     mixed_ref[...] = half(wide(xv[...]) + total)
     mixed_store.start()
 
-    late.y_to_z()
-    early.all_to_y()
+    late.y_to_near()
+    late.near_to_far()
+    early.far_to_all()
 
     total = wide(gns[p.head])
     for step in (1, 2, 3):
@@ -675,7 +694,8 @@
     gx_ref[...] = half(wide(gg[p.head]) + d_input)
     gx_store.start()
 
-    late.z_to_all()
+    early.all_to_y()
+    late.far_to_all()
     early.y_to_core()
     for spread_copy in (normed_gather, grad_gather, out_spread, norm_spread):
         spread_copy.wait_sent()
@@ -683,13 +703,15 @@
         one.wait_sent()
     late.all_to_y()
     early.finish()
-    take(early.res, T, 0, gwo_ref, 0, 192)
-    take(early.res, T, 192, gqkv_ref, 0, 192)
+    take(early.res, 0, gwo_ref, 0, 192)
+    take(early.res, 192, gqkv_ref, 0, 192)
     gwo_store.start()
     query_store.start()
     late.y_to_core()
+    early.wait_sent()
     late.finish()
-    take(late.res, T, 0, gqkv_ref, 192, 384)
+    late.wait_sent()
+    take(late.res, 0, gqkv_ref, 192, 384)
     rest_store.start()
     for store in (mixed_store, gx_store, gwo_store, query_store, rest_store):
         store.wait()
@@ -755,8 +777,8 @@
             around,
             around,
             around,
-            *Summed.scratch(T),
-            *Summed.scratch(T),
+            *Summed.scratch(),
+            *Summed.scratch(),
         ],
         compiler_params=pltpu.CompilerParams(
             collective_id=0, has_side_effects=True, vmem_limit_bytes=63 * 2**20

time: 82.5 us -> 74.7 us (0.905)
  Pallas kernels: 81.7 us -> 73.9 us
    pallas_call x1, Pallas kernels: 79.4 us -> 71.6 us  [on_device(): pl.pallas_call(block_kernel, out_shape=[jax.ShapeDtypeStruct((CELLS, FULL...]
where the time goes in v4:
time: 74.7 us; the launch traced here: 74.6 us
  Pallas kernels  73.9 us (99%)
    pallas_call x1, Pallas kernels, on_device(): pl.pallas_call(block_kernel, out_shape=[jax.ShapeDtypeStruct((CELLS, FULL...  71.6 us
    pallas_call x1, Pallas kernels, on_device(): pl.pallas_call(store_kernel, out_shape=[jax.ShapeDtypeStruct(result.shape...  2.35 us

profile of v4, /device:TPU:1, one launch (start us, length us, event | category | flops | bytes accessed | tf_op | source)
XLA Modules:
  0.0 74.6 jit_solution(6200287430779813921)
XLA Ops:
  0.6 71.6 %shard_map.84 = (bf16[64,768]{1,0:T(8,128)(2,1)}, bf16[64,768]{1,0:T(8,128)(2,1)}, bf16[576,768]{1,0:T(8,128)(2,1)}, bf16[192,768]{1,0:T(8,128)(2,1)}) custom-call(bf16[64,768]{1,0:T(8,128)(2,1)} %bitcast.5, bf16[64,768]{1,0:T(8,128)(2,1)} %bitcast.6, bf16[3,192,768]{2,1,0:T(8,128)(2,1)} %wqkv_ref.1, bf16[192,768]{1,0:T(8,128)(2,1)} %wo_ref.1, s32[8,32]{1,0:T(8,128)} %valid_ref.1), custom_call_target="tpu_custom_call" | custom-call | tf_op jit(solution)/shard_map/pallas_call | solution.py:738
  72.2 2.4 %shard_map.85 = (bf16[64,768]{1,0:T(8,128)(2,1)}, bf16[64,768]{1,0:T(8,128)(2,1)}, bf16[576,768]{1,0:T(8,128)(2,1)}, bf16[192,768]{1,0:T(8,128)(2,1)}) custom-call(bf16[64,768]{1,0:T(8,128)(2,1)} %get-tuple-element.12.refs_0_, bf16[64,768]{1,0:T(8,128)(2,1)} %get-tuple-element.13.refs_1_, bf16[576,768]{1,0:T(8,128)(2,1)} %get-tuple-element.14.refs_2_, ...), custom_call_target="tpu_custom_call" | custom-call | tf_op jit(solution)/shard_map/pallas_call | solution.py:793

commit v5 on v4

--- a/solution.py
+++ b/solution.py
@@ -382,7 +382,7 @@
 
 def block_kernel(
     x_ref, gy_ref, wqkv_ref, wo_ref, valid_ref, mixed_out, gx_out, gqkv_out, gwo_out,
-    mixed_ref, gx_ref, gqkv_ref, gwo_ref, sem_out, xv, valid_v, ng, gg, norm32, spread, wp, wop, ext, dext, stats, mask_q, mask_k, gp, pvs, pvr, gns, gnr,
+    mixed_ref, gx_ref, gqkv_ref, gwo_ref, soft_v, soft_grad_v, sem_out, xv, valid_v, ng, gg, norm32, spread, wp, wop, ext, dext, stats, mask_q, mask_k, gp, pvs, pvr, gns, gnr,
     sem_in, sem_n, sem_g, sem_pv, sem_gn, sem_ext, sem_dext, sem_stats, *sums,
 ):
     p = Place()
@@ -406,8 +406,8 @@
         )
     ]
 
-    query_rows, rest = pl.ds(0, 192), pl.ds(192, 384)
-    mixed_store, gx_store, gwo_store, query_store, rest_store = [
+    query_rows = pl.ds(0, 192)
+    mixed_store, gx_store, gwo_store, query_store = [
         pltpu.make_async_copy(src, dst, sem_out.at[index])
         for index, (src, dst) in enumerate(
             (
@@ -415,7 +415,6 @@
                 (gx_ref, gx_out),
                 (gwo_ref, gwo_out),
                 (gqkv_ref.at[query_rows], gqkv_out.at[query_rows]),
-                (gqkv_ref.at[rest], gqkv_out.at[rest]),
             )
         )
     ]
@@ -593,11 +592,8 @@
         inner = dot_rows(douts, values)
         carried = jnp.sum(chance * inner, axis=1, keepdims=True)
         soft_grad = half(chance * (inner - carried))
-        attended = dot(half(chance), values)
-        grad_query = dot(soft_grad, keys) * HEAD_SIZE ** (-0.5)
-        gp[block, :, 640:768] = half(jnp.where(low, attended[0:64, 0:128], attended[64:128, 0:128]))
-        gp[block, :, 0:128] = half(jnp.where(low, grad_query[0:64, 0:128], grad_query[64:128, 0:128]))
-        gp[block, :, 384:512] = half(jnp.where(low, grad_query[128:192, 128:256], attended[128:192, 128:256]))
+        soft_v[block] = half(chance)
+        soft_grad_v[block] = soft_grad
         tile = jnp.zeros((CELLS, 128), jnp.float32)
         for kind, column in enumerate((level, carried)):
             for head in range(3):
@@ -608,9 +604,19 @@
                     tile = jnp.where(lane == 9 * kind + 3 * head + digit, piece, tile)
         stats[block + 1, 48:112] = half(tile)
 
+    def queries_rest(block):
+        keys, values = around(block, K01, KV2), around(block, V01, KV2)
+        attended = dot(soft_v[block], values)
+        grad_query = dot(soft_grad_v[block], keys) * HEAD_SIZE ** (-0.5)
+        gp[block, :, 640:768] = half(jnp.where(low, attended[0:64, 0:128], attended[64:128, 0:128]))
+        gp[block, :, 0:128] = half(jnp.where(low, grad_query[0:64, 0:128], grad_query[64:128, 0:128]))
+        gp[block, :, 384:512] = half(jnp.where(low, grad_query[128:192, 128:256], attended[128:192, 128:256]))
+
     for block in range(4):
         queries_side(block)
     stat_halo.send_all()
+    for block in range(4):
+        queries_rest(block)
 
     def cells(ref, *groups):
         return jnp.concatenate([ref[:, :, g * 128 : g * 128 + 128].reshape(4 * CELLS, 128) for g in groups], axis=1)
@@ -662,13 +668,18 @@
     late.send_core()
     early.y_to_near()
 
+    late.core_to_y()
+
     norm_spread = Spread(p, gns, gnr, sem_gn)
     gns[...] = half(dot(cells(gp, 0, 1, 2, 3, 4), wp[...])).reshape(4, CELLS, FULL)
     for step in (2, 1, 3):
         norm_spread.copy(norm_spread.other(step)).start()
 
-    late.core_to_y()
     early.near_to_far()
+
+    late.y_to_near()
+    late.near_to_far()
+    early.far_to_all()
 
     total = wide(pvs[p.head])
     for step in (1, 2, 3):
@@ -677,10 +688,6 @@
         total = total + wide(pvr[other])
     mixed_ref[...] = half(wide(xv[...]) + total)
     mixed_store.start()
-
-    late.y_to_near()
-    late.near_to_far()
-    early.far_to_all()
 
     total = wide(gns[p.head])
     for step in (1, 2, 3):
@@ -693,6 +700,7 @@
     d_input = spread[:, 0:1] * (total - mean - own_norm * along)
     gx_ref[...] = half(wide(gg[p.head]) + d_input)
     gx_store.start()
+
 
     early.all_to_y()
     late.far_to_all()
@@ -709,11 +717,21 @@
     query_store.start()
     late.y_to_core()
     early.wait_sent()
-    late.finish()
+    quarters = []
+    for step in (0, 1, 3, 2):
+        y = lax.rem(p.y + step, N_Y)
+        late.cg_copy(y, True).wait_recv()
+        for third in range(6):
+            to = pl.ds(pl.multiple_of(192 + 96 * y + 16 * third, 16), 16)
+            for column in range(6):
+                gqkv_ref[to, column * 128 : column * 128 + 128] = late.res[
+                    column // 3, y, third * 3 + column % 3
+                ]
+        to = pl.ds(pl.multiple_of(192 + 96 * y, 16), 96)
+        quarters.append(pltpu.make_async_copy(gqkv_ref.at[to], gqkv_out.at[to], sem_out.at[4 + step]))
+        quarters[-1].start()
     late.wait_sent()
-    take(late.res, 0, gqkv_ref, 192, 384)
-    rest_store.start()
-    for store in (mixed_store, gx_store, gwo_store, query_store, rest_store):
+    for store in (mixed_store, gx_store, gwo_store, query_store, *quarters):
         store.wait()
 
 
@@ -750,7 +768,9 @@
             pltpu.VMEM((CELLS, FULL), bf),
             pltpu.VMEM((3 * 192, FULL), bf),
             pltpu.VMEM((192, FULL), bf),
-            pltpu.SemaphoreType.DMA((5,)),
+            pltpu.VMEM((4, 192, AROUND), bf),
+            pltpu.VMEM((4, 192, AROUND), bf),
+            pltpu.SemaphoreType.DMA((8,)),
             pltpu.VMEM((CELLS, FULL), bf),
             pltpu.VMEM((8, N_LON), jnp.int32),
             gathered,

time: 74.7 us -> 73.5 us (0.984)
  Pallas kernels: 73.9 us -> 72.7 us
    pallas_call x1, Pallas kernels: 71.6 us -> 70.3 us  [on_device(): pl.pallas_call(block_kernel, out_shape=[jax.ShapeDtypeStruct((CELLS, FULL...]
where the time goes in v5:
time: 73.5 us; the launch traced here: 73.3 us
  Pallas kernels  72.7 us (99%)
    pallas_call x1, Pallas kernels, on_device(): pl.pallas_call(block_kernel, out_shape=[jax.ShapeDtypeStruct((CELLS, FULL...  70.3 us
    pallas_call x1, Pallas kernels, on_device(): pl.pallas_call(store_kernel, out_shape=[jax.ShapeDtypeStruct(result.shape...  2.35 us

profile of v5, /device:TPU:1, one launch (start us, length us, event | category | flops | bytes accessed | tf_op | source)
XLA Modules:
  0.0 73.3 jit_solution(18053626788001968548)
XLA Ops:
  0.6 70.3 %shard_map.84 = (bf16[64,768]{1,0:T(8,128)(2,1)}, bf16[64,768]{1,0:T(8,128)(2,1)}, bf16[576,768]{1,0:T(8,128)(2,1)}, bf16[192,768]{1,0:T(8,128)(2,1)}) custom-call(bf16[64,768]{1,0:T(8,128)(2,1)} %bitcast.5, bf16[64,768]{1,0:T(8,128)(2,1)} %bitcast.6, bf16[3,192,768]{2,1,0:T(8,128)(2,1)} %wqkv_ref.1, bf16[192,768]{1,0:T(8,128)(2,1)} %wo_ref.1, s32[8,32]{1,0:T(8,128)} %valid_ref.1), custom_call_target="tpu_custom_call" | custom-call | tf_op jit(solution)/shard_map/pallas_call | solution.py:756
  70.9 2.4 %shard_map.85 = (bf16[64,768]{1,0:T(8,128)(2,1)}, bf16[64,768]{1,0:T(8,128)(2,1)}, bf16[576,768]{1,0:T(8,128)(2,1)}, bf16[192,768]{1,0:T(8,128)(2,1)}) custom-call(bf16[64,768]{1,0:T(8,128)(2,1)} %get-tuple-element.12.refs_0_, bf16[64,768]{1,0:T(8,128)(2,1)} %get-tuple-element.13.refs_1_, bf16[576,768]{1,0:T(8,128)(2,1)} %get-tuple-element.14.refs_2_, ...), custom_call_target="tpu_custom_call" | custom-call | tf_op jit(solution)/shard_map/pallas_call | solution.py:813

commit v6 on v5

--- a/solution.py
+++ b/solution.py
@@ -382,7 +382,7 @@
 
 def block_kernel(
     x_ref, gy_ref, wqkv_ref, wo_ref, valid_ref, mixed_out, gx_out, gqkv_out, gwo_out,
-    mixed_ref, gx_ref, gqkv_ref, gwo_ref, soft_v, soft_grad_v, sem_out, xv, valid_v, ng, gg, norm32, spread, wp, wop, ext, dext, stats, mask_q, mask_k, gp, pvs, pvr, gns, gnr,
+    mixed_ref, gx_ref, gqkv_ref, gwo_ref, wpt, wopt, soft_v, soft_grad_v, sem_out, xv, valid_v, ng, gg, norm32, spread, wp, wop, ext, dext, stats, mask_q, mask_k, gp, pvs, pvr, gns, gnr,
     sem_in, sem_n, sem_g, sem_pv, sem_gn, sem_ext, sem_dext, sem_stats, *sums,
 ):
     p = Place()
@@ -422,7 +422,7 @@
     def greet(device):
         pl.semaphore_signal(barrier, inc=1, device_id=device, device_id_type=MESH)
 
-    for load in loads:
+    for load in loads[:3]:
         load.start()
     for step in range(1, N_HEAD):
         greet(p.peer(lax.rem(p.head + step, N_HEAD)))
@@ -459,19 +459,14 @@
     norm32[...] = center * inv
     spread[...] = jnp.broadcast_to(inv, spread.shape)
     ng[p.head] = half(center * inv)
-    for top, at_edge in ((0, p.lat == 0), (112, p.lat == N_LAT - 1)):
-
-        @pl.when(at_edge)
-        def _():
-            for ref in (ext, dext, stats):
-                ref[:, top : top + 48, :] = jnp.zeros((6, 48, ref.shape[2]), jnp.bfloat16)
-
     greeted = 3 + 2 + (N_Y - 1) + 7
     edge = jnp.where(p.lat > 0, 3, 0) + jnp.where(p.lat < N_LAT - 1, 3, 0)
     pl.semaphore_wait(barrier, greeted + edge)
 
     for step in (1, 3, 2):
         normed_gather.copy(normed_gather.other(step)).start()
+    for load in loads[3:]:
+        load.start()
     loads[2].wait()
     for step in (1, 3, 2):
         grad_gather.copy(grad_gather.other(step)).start()
@@ -496,12 +491,21 @@
         ext[block + 1, 48:112, 512:640] = half(flag)
         mask_k[block] = jnp.where(inside_rows & ((flag[:, 0:1] > 0) | middle), 0.0, NEGATIVE)
 
+    for top, at_edge in ((0, p.lat == 0), (112, p.lat == N_LAT - 1)):
+
+        @pl.when(at_edge)
+        def _():
+            for ref in (ext, dext, stats):
+                ref[:, top : top + 48, :] = jnp.zeros((6, 48, ref.shape[2]), jnp.bfloat16)
+
     early.clear()
     late.clear()
     wp[448:512] = jnp.zeros((64, FULL), jnp.bfloat16)
     wop[128:192] = jnp.zeros((64, FULL), jnp.bfloat16)
     for load in loads[3:]:
         load.wait()
+    wpt[...] = wp[...].T
+    wopt[...] = wop[...].T
 
     def first(values):
         return jnp.where(low, values, zero)
@@ -529,7 +533,7 @@
             margins.send_side(1)
 
     def project_normed(block):
-        projected = dot_rows(ng[block], wp[...])
+        projected = dot(ng[block], wpt[...])
         scale = HEAD_SIZE ** (-0.5)
         ext[block + 1, 48:112, 0:128] = half(half(projected[:, 0:128]) * scale)
         ext[block + 1, 48:112, 128:384] = half(projected[:, 128:384])
@@ -539,7 +543,7 @@
         )
 
     def project_grad(block):
-        dext[block + 1, 48:112] = half(dot_rows(gg[block], wop[...]))
+        dext[block + 1, 48:112] = half(dot(gg[block], wopt[...]))
 
     @pl.loop(0, N_HEAD)
     def _(step):
@@ -768,6 +772,8 @@
             pltpu.VMEM((CELLS, FULL), bf),
             pltpu.VMEM((3 * 192, FULL), bf),
             pltpu.VMEM((192, FULL), bf),
+            pltpu.VMEM((FULL, 640), bf),
+            pltpu.VMEM((FULL, 256), bf),
             pltpu.VMEM((4, 192, AROUND), bf),
             pltpu.VMEM((4, 192, AROUND), bf),
             pltpu.SemaphoreType.DMA((8,)),

time: 73.5 us -> 73.2 us (level)
  no operation moved by 1% of the time
where the time goes in v6:
time: 73.2 us; the launch traced here: 73 us
  Pallas kernels  72.3 us (99%)
    pallas_call x1, Pallas kernels, on_device(): pl.pallas_call(block_kernel, out_shape=[jax.ShapeDtypeStruct((CELLS, FULL...  70 us
    pallas_call x1, Pallas kernels, on_device(): pl.pallas_call(store_kernel, out_shape=[jax.ShapeDtypeStruct(result.shape...  2.35 us

profile of v6, /device:TPU:1, one launch (start us, length us, event | category | flops | bytes accessed | tf_op | source)
XLA Modules:
  0.0 73.0 jit_solution(13460036089726251996)
XLA Ops:
  0.6 70.0 %shard_map.84 = (bf16[64,768]{1,0:T(8,128)(2,1)}, bf16[64,768]{1,0:T(8,128)(2,1)}, bf16[576,768]{1,0:T(8,128)(2,1)}, bf16[192,768]{1,0:T(8,128)(2,1)}) custom-call(bf16[64,768]{1,0:T(8,128)(2,1)} %bitcast.5, bf16[64,768]{1,0:T(8,128)(2,1)} %bitcast.6, bf16[3,192,768]{2,1,0:T(8,128)(2,1)} %wqkv_ref.1, bf16[192,768]{1,0:T(8,128)(2,1)} %wo_ref.1, s32[8,32]{1,0:T(8,128)} %valid_ref.1), custom_call_target="tpu_custom_call" | custom-call | tf_op jit(solution)/shard_map/pallas_call | solution.py:760
  70.6 2.4 %shard_map.85 = (bf16[64,768]{1,0:T(8,128)(2,1)}, bf16[64,768]{1,0:T(8,128)(2,1)}, bf16[576,768]{1,0:T(8,128)(2,1)}, bf16[192,768]{1,0:T(8,128)(2,1)}) custom-call(bf16[64,768]{1,0:T(8,128)(2,1)} %get-tuple-element.12.refs_0_, bf16[64,768]{1,0:T(8,128)(2,1)} %get-tuple-element.13.refs_1_, bf16[576,768]{1,0:T(8,128)(2,1)} %get-tuple-element.14.refs_2_, ...), custom_call_target="tpu_custom_call" | custom-call | tf_op jit(solution)/shard_map/pallas_call | solution.py:819

commit v7 on v6

--- a/solution.py
+++ b/solution.py
@@ -635,10 +635,6 @@
     put(early.src, 192, weights[0:192])
     early.send_core()
 
-    out_spread = Spread(p, pvs, pvr, sem_pv)
-    pvs[...] = half(dot(mixed_in, wop[...])).reshape(4, CELLS, FULL)
-    for step in (2, 1, 3):
-        out_spread.copy(out_spread.other(step)).start()
     early.core_to_y()
     stat_halo.wait_all()
 
@@ -679,6 +675,10 @@
     for step in (2, 1, 3):
         norm_spread.copy(norm_spread.other(step)).start()
 
+    out_spread = Spread(p, pvs, pvr, sem_pv)
+    pvs[...] = half(dot(mixed_in, wop[...])).reshape(4, CELLS, FULL)
+    for step in (2, 1, 3):
+        out_spread.copy(out_spread.other(step)).start()
     early.near_to_far()
 
     late.y_to_near()

time: 73.2 us -> 73.5 us (level)
  no operation moved by 1% of the time
where the time goes in v7:
time: 73.5 us; the launch traced here: 73.1 us
  Pallas kernels  72.5 us (99%)
    pallas_call x1, Pallas kernels, on_device(): pl.pallas_call(block_kernel, out_shape=[jax.ShapeDtypeStruct((CELLS, FULL...  70.1 us
    pallas_call x1, Pallas kernels, on_device(): pl.pallas_call(store_kernel, out_shape=[jax.ShapeDtypeStruct(result.shape...  2.35 us

profile of v7, /device:TPU:1, one launch (start us, length us, event | category | flops | bytes accessed | tf_op | source)
XLA Modules:
  0.0 73.1 jit_solution(9836204005185854079)
XLA Ops:
  0.6 70.1 %shard_map.84 = (bf16[64,768]{1,0:T(8,128)(2,1)}, bf16[64,768]{1,0:T(8,128)(2,1)}, bf16[576,768]{1,0:T(8,128)(2,1)}, bf16[192,768]{1,0:T(8,128)(2,1)}) custom-call(bf16[64,768]{1,0:T(8,128)(2,1)} %bitcast.5, bf16[64,768]{1,0:T(8,128)(2,1)} %bitcast.6, bf16[3,192,768]{2,1,0:T(8,128)(2,1)} %wqkv_ref.1, bf16[192,768]{1,0:T(8,128)(2,1)} %wo_ref.1, s32[8,32]{1,0:T(8,128)} %valid_ref.1), custom_call_target="tpu_custom_call" | custom-call | tf_op jit(solution)/shard_map/pallas_call | solution.py:760
  70.8 2.4 %shard_map.85 = (bf16[64,768]{1,0:T(8,128)(2,1)}, bf16[64,768]{1,0:T(8,128)(2,1)}, bf16[576,768]{1,0:T(8,128)(2,1)}, bf16[192,768]{1,0:T(8,128)(2,1)}) custom-call(bf16[64,768]{1,0:T(8,128)(2,1)} %get-tuple-element.12.refs_0_, bf16[64,768]{1,0:T(8,128)(2,1)} %get-tuple-element.13.refs_1_, bf16[576,768]{1,0:T(8,128)(2,1)} %get-tuple-element.14.refs_2_, ...), custom_call_target="tpu_custom_call" | custom-call | tf_op jit(solution)/shard_map/pallas_call | solution.py:819
